TPU v7x, 32 devices: a whole 2x2x4 slice. The times are simulated.
32 devices in a mesh: grp: 2 (over x), blk: 8 (over z, y), face: 2 (over core).
Axes of the slice: x: 2, y: 2, z: 4, core: 2. Of those that a mesh axis runs over, the one named last changes fastest.
Arguments:
- record: float32 [8192, 4096], P('blk', ('grp', 'face')), parts along dimension 1
- face_area: int32 [2048], P('face'), may hold values from 4 to 64
- face_tap: int32 [2048], P('face'), may hold values from 0 to 511
- lever_table: int32 [512, 3], replicated, may hold values from -4 to 4
- start_modes: float32 [2, 16, 16, 4], replicated, may hold values from -6 to 6
Outputs:
- cross_spectra: float32 [2, 32, 16, 16], P(None, 'grp', 'blk'), parts along dimension 1
- modal_forces: float32 [2, 32, 4, 3], P(None, 'grp'), parts along dimension 1
There are 2 independent parts, one for each index of `grp`. A program takes and returns all parts, laid end to end along the dimension named above; an argument that names none is the same for every part. Nothing has to cross between parts.
All inputs are finite; a program needn't handle non-finite values.
Results may differ from a plain program's by a relative error of at most 0.0001.
Values sent between devices are 32-bit elements; how exact they have to be, the bound alone decides.
No kernel may reach another device: no remote copies, remote signals or barrier semaphores. Data moves between devices by JAX's collectives and lax.ppermute only.
A program may use at most 64 MiB of HBM per device.

v0:
```python
import math

import jax
import jax.numpy as jnp
from jax import lax
from jax.sharding import PartitionSpec as P

NFFT = 1024
HOP = 512
BIN = 16
FIRST_BIN = 24
PITERS = 2
BLK_DEV = 2
NTAP = 512


HIGH = lax.Precision.HIGHEST


def shifted(x, axis, by):
    count = lax.axis_size(axis)
    return lax.ppermute(x, axis, [(i, (i + by) % count) for i in range(count)])


def band_twiddle():
    steps = jnp.arange(NFFT, dtype=jnp.int32)
    bins = FIRST_BIN + jnp.arange(BIN, dtype=jnp.int32)
    angle = (steps[:, None] * bins[None, :] % NFFT).astype(jnp.float32) * (2.0 * math.pi / NFFT)
    window = 0.5 - 0.5 * jnp.cos(steps.astype(jnp.float32) * (2.0 * math.pi / NFFT))
    scaling = jnp.sqrt(jnp.sum(window * window))
    cosine = window[:, None] * jnp.cos(angle) / scaling
    sine = -window[:, None] * jnp.sin(angle) / scaling
    return jnp.concatenate([cosine, sine], axis=1)


def gram_tiles(weighted, others):
    real_tile = jnp.einsum("kif,kjf->kij", weighted[0], others[0], precision=HIGH)
    real_tile = real_tile + jnp.einsum("kif,kjf->kij", weighted[1], others[1], precision=HIGH)
    imag_tile = jnp.einsum("kif,kjf->kij", weighted[0], others[1], precision=HIGH)
    imag_tile = imag_tile - jnp.einsum("kif,kjf->kij", weighted[1], others[0], precision=HIGH)
    return jnp.stack([real_tile, imag_tile])


def apply_gram(gram_part, modes_re, modes_im):
    new_re = jnp.einsum("kij,kjm->kim", gram_part[0], modes_re, precision=HIGH) - jnp.einsum(
        "kij,kjm->kim", gram_part[1], modes_im, precision=HIGH
    )
    new_im = jnp.einsum("kij,kjm->kim", gram_part[0], modes_im, precision=HIGH) + jnp.einsum(
        "kij,kjm->kim", gram_part[1], modes_re, precision=HIGH
    )
    return (new_re, new_im)


def on_device(record, face_area, face_tap, lever_table, start_modes):
    face_count = record.shape[1]
    cycle_size = lax.axis_size("blk")
    block_count = BLK_DEV * cycle_size
    total_faces = face_count * lax.axis_size("face")
    twiddle = band_twiddle()
    first_hop = record[:HOP]
    following = shifted(first_hop, "blk", -1)
    extended = jnp.concatenate([record, following], axis=0).reshape(BLK_DEV + 1, HOP, face_count)
    spectra = jnp.einsum("tk,btf->kbf", twiddle[:HOP], extended[:BLK_DEV], precision=HIGH)
    spectra = spectra + jnp.einsum("tk,btf->kbf", twiddle[HOP:], extended[1:], precision=HIGH)
    panels = jnp.stack([spectra[:BIN], spectra[BIN:]])
    weight = face_area.astype(jnp.float32) / 64.0
    weighted = panels * weight
    contrib = gram_tiles(weighted, lax.all_gather(panels, "blk", axis=2, tiled=True))
    gram_rows = contrib
    gram_rows = lax.psum(gram_rows, "face") / total_faces
    modes_re = start_modes[0]
    modes_im = start_modes[1]
    for sweep_index in range(PITERS):
        rows_re, rows_im = apply_gram(gram_rows, modes_re, modes_im)
        squares = lax.psum(jnp.sum(rows_re * rows_re + rows_im * rows_im, axis=1), "blk")
        column_scale = jnp.sqrt(squares / block_count + 1e-06)[:, None, :]
        rows_re = rows_re / column_scale
        rows_im = rows_im / column_scale
        if sweep_index + 1 < PITERS:
            gathered = lax.all_gather(jnp.stack([rows_re, rows_im]), "blk", axis=2, tiled=True)
            modes_re = gathered[0]
            modes_im = gathered[1]
    onehot = (face_tap[:, None] == jnp.arange(NTAP, dtype=jnp.int32)[None, :]).astype(jnp.float32)
    face_weight = weight[:, None] * jnp.dot(onehot, lever_table.astype(jnp.float32), precision=HIGH)
    force_norm = math.sqrt(total_faces * block_count)
    load_re = jnp.einsum("kbf,fc->kbc", panels[0], face_weight, precision=HIGH) / force_norm
    load_im = jnp.einsum("kbf,fc->kbc", panels[1], face_weight, precision=HIGH) / force_norm
    force_re = jnp.einsum("kbc,kbm->kmc", load_re, rows_re, precision=HIGH) - jnp.einsum(
        "kbc,kbm->kmc", load_im, rows_im, precision=HIGH
    )
    force_im = jnp.einsum("kbc,kbm->kmc", load_re, rows_im, precision=HIGH) + jnp.einsum(
        "kbc,kbm->kmc", load_im, rows_re, precision=HIGH
    )
    modal_forces = lax.psum(jnp.stack([force_re, force_im]), ("blk", "face"))
    return (gram_rows, modal_forces)


def solution(mesh):
    return jax.shard_map(
        on_device,
        mesh=mesh,
        in_specs=(P("blk", ("grp", "face")), P("face"), P("face"), P(), P()),
        out_specs=(P(None, "grp", "blk", None), P(None, "grp", None, None)),
        check_vma=False,
    )
```

profile of v0, /device:TPU:0, one launch (start us, length us, event | category | flops | bytes accessed | tf_op | source)
XLA Modules:
  0.0 265.4 jit_solution(5762455616327423982)
XLA Ops:
  7.2 0.0 all-gather.2.cloned.1.call-start
  7.2 3.2 %slice.68 = f32[512,1024]{1,0:T(8,128)} slice(f32[1024,1024]{1,0:T(8,128)} %param.5), slice={[0:512], [0:1024]} | slice | bytes 4194304 | tf_op jit(solution)/shard_map/slice | solution.py:60
  10.4 6.0 %collective-permute-start = (f32[512,1024]{1,0:T(8,128)}, f32[512,1024]{1,0:T(8,128)S(1)}, u32[]{:S(2)}, u32[]{:S(2)}) collective-permute-start(f32[512,1024]{1,0:T(8,128)} %slice.68), channel_id=1, source_target_pairs={{0,14},{2,0},{4,2},{6,4},{8,6},{10,8},{12,10},{14,12},{1,15},{3,1}... | collective-permute-start | bytes 6291464 | tf_op jit(solution)/shard_map/ppermute | solution.py:22
  16.4 0.6 multiply_reduce_fusion
  17.9 0.3 multiply_divide_fusion
  18.2 4.9 %fusion.25 = f32[32,2,1024]{2,0,1:T(8,128)S(1)} fusion(f32[2,512,1024]{2,1,0:T(8,128)} %bitcast.80, f32[1024,16]{0,1:T(8,128)S(1)} %get-tuple-element.17, f32[1024,16]{0,1:T(8,128)S(1)} %get-tuple-element.16), kind=kOutput, calls=%fused_computation.51 | convolution fusion | flops 402669568 | bytes 4587520 | tf_op jit(solution)/shard_map/tk,btf->kbf/dot_general | solution.py:63
  23.1 38.5 %collective-permute-done = f32[512,1024]{1,0:T(8,128)S(1)} collective-permute-done((f32[512,1024]{1,0:T(8,128)}, f32[512,1024]{1,0:T(8,128)S(1)}, u32[]{:S(2)}, u32[]{:S(2)}) %collective-permute-start) | collective-permute-done | bytes 2097184 | tf_op jit(solution)/shard_map/ppermute | solution.py:22
  61.6 0.6 pad_maximum_fusion
  62.2 0.0 copy-start.4
  62.2 0.0 copy-start.5
  62.2 2.5 convolution_add_fusion
  64.7 0.8 broadcast_multiply_fusion
  65.5 0.0 all-gather.2.cloned.1.call-update
  65.6 1.1 fusion.4
  66.6 0.6 convolution_multiply_fusion.1
  67.2 0.1 copy.37
  67.3 0.6 convolution_multiply_fusion
  67.9 0.1 copy.38
  68.0 48.7 %all-gather.2.cloned.1.call-done = f32[2,16,16,1024]{3,1,2,0:T(8,128)} async-done(((f32[2,16,2,1024]{3,1,2,0:T(8,128)}), f32[2,16,16,1024]{3,1,2,0:T(8,128)}) %all-gather.2.cloned.1.call-update) | async-done | bytes 2097168 | tf_op jit(solution)/shard_map/all_gather | solution.py:68
  116.7 1.7 slice_bitcast_fusion.1
  118.4 1.9 fusion.12
  120.3 1.9 fusion.8
  122.2 1.9 fusion.6
  124.1 2.1 fusion.5
  126.2 3.4 %psum.28 = f32[2,16,2,16]{3,2,1,0:T(2,128)S(1)} all-reduce(f32[2,16,2,16]{3,2,1,0:T(2,128)S(1)} %pad_maximum_fusion.3), channel_id=1, replica_groups=mesh['grp'=2,'blk'=8,'face'=2] {'face'}, use_global_device_ids=true, to_apply=%region_1.2 | all-reduce | flops 1024 | bytes 8192 | tf_op jit(solution)/shard_map/psum | solution.py:70
  129.7 0.0 copy-start.1
  129.7 0.2 fusion.43
  130.0 0.2 fusion.39
  130.2 0.2 convolution_subtract_fusion.2
  130.5 0.3 add_reduce_fusion.1
  130.7 19.2 %psum.29 = f32[16,4]{1,0:T(8,128)S(1)} all-reduce(f32[16,4]{1,0:T(8,128)S(1)} %get-tuple-element.18), channel_id=1, replica_groups=mesh['grp'=2,'blk'=8,'face'=2] {'blk'}, use_global_device_ids=true, to_apply=%region_3.4 | all-reduce | flops 64 | bytes 512 | tf_op jit(solution)/shard_map/psum | solution.py:75
  150.0 0.1 copy.32
  150.0 0.1 copy.33
  150.2 30.5 %all_gather.7 = f32[2,16,16,4]{1,3,0,2:T(4,128)S(1)} all-gather(f32[2,16,2,4]{1,3,0,2:T(4,128)S(1)} %copy.34), channel_id=1, replica_groups=mesh['grp'=2,'blk'=8,'face'=2] {'blk'}, dimensions={2}, use_global_device_ids=true | all-gather | bytes 9216 | tf_op jit(solution)/shard_map/all_gather | solution.py:80
  180.7 0.1 copy.44
  180.7 0.2 fusion.33
  181.0 0.1 copy.43
  181.1 0.2 fusion.37
  181.3 0.2 convolution_subtract_fusion.1
  181.6 0.3 add_reduce_fusion
  181.9 17.6 %psum.30 = f32[16,4]{1,0:T(8,128)S(1)} all-reduce(f32[16,4]{1,0:T(8,128)S(1)} %get-tuple-element.20), channel_id=1, replica_groups=mesh['grp'=2,'blk'=8,'face'=2] {'blk'}, use_global_device_ids=true, to_apply=%region_5.6 | all-reduce | flops 64 | bytes 512 | tf_op jit(solution)/shard_map/psum | solution.py:75
  199.5 0.3 fusion.53
  199.8 0.3 fusion.54
  200.1 0.3 fusion.2
  200.4 0.1 copy.41
  200.5 0.3 fusion.1
  200.8 0.1 copy.42
  200.9 57.6 %psum.31 = f32[2,16,4,3]{1,2,3,0:T(4,128)} all-reduce(f32[2,16,4,3]{1,2,3,0:T(4,128)S(1)} %pad_maximum_fusion.4), channel_id=1, replica_groups=mesh['grp'=2,'blk'=8,'face'=2] {'blk','face'}, use_global_device_ids=true, to_apply=%region_6.7 | all-reduce | flops 384 | bytes 3072 | tf_op jit(solution)/shard_map/psum | solution.py:94
  (23 shorter events, 0.2 us)
Async XLA Ops:
  7.2 10.7 %copy-start.3 = (s32[1024]{0:T(1024)S(1)}, s32[1024]{0:T(1024)}, u32[]{:S(2)}) copy-start(s32[1024]{0:T(1024)} %param.6) | copy-start | bytes 12292
  7.2 109.6 %all-gather.2.cloned.1.call-start = ((), (), s32[]{:S(2)}) async-start(), calls=%async_computation | async-start | bytes 2359296 | tf_op jit(solution)/shard_map/all_gather | solution.py:68
  10.4 51.2 %collective-permute-start = (f32[512,1024]{1,0:T(8,128)}, f32[512,1024]{1,0:T(8,128)S(1)}, u32[]{:S(2)}, u32[]{:S(2)}) collective-permute-start(f32[512,1024]{1,0:T(8,128)} %slice.68), channel_id=1, source_target_pairs={{0,14},{2,0},{4,2},{6,4},{8,6},{10,8},{12,10},{14,12},{1,15},{3,1}... | collective-permute-start | bytes 6291464 | tf_op jit(solution)/shard_map/ppermute | solution.py:22
  17.8 43.9 %copy-start = (f32[1024,1024]{1,0:T(8,128)S(1)}, f32[1024,1024]{1,0:T(8,128)}, u32[]{:S(2)}) copy-start(f32[1024,1024]{1,0:T(8,128)} %param.5) | copy-start | bytes 12582916
  62.2 3.3 %copy-start.4 = (s32[512,3]{0,1:T(4,128)S(1)}, s32[512,3]{0,1:T(4,128)}, u32[]{:S(2)}) copy-start(s32[512,3]{0,1:T(4,128)} %param.8) | copy-start | bytes 18436
  62.2 3.3 %copy-start.5 = (s32[1024]{0:T(1024)S(1)}, s32[1024]{0:T(1024)}, u32[]{:S(2)}) copy-start(s32[1024]{0:T(1024)} %param.7) | copy-start | bytes 12292
  68.0 61.7 %copy-start.2 = (f32[2,16,16,4]{2,3,1,0:T(4,128)S(1)}, f32[2,16,16,4]{2,3,1,0:T(4,128)}, u32[]{:S(2)}) copy-start(f32[2,16,16,4]{2,3,1,0:T(4,128)} %param.9) | copy-start | bytes 24580
  129.7 128.8 %copy-start.1 = (f32[2,16,2,16]{3,2,1,0:T(2,128)}, f32[2,16,2,16]{3,2,1,0:T(2,128)S(1)}, u32[]{:S(2)}) copy-start(f32[2,16,2,16]{3,2,1,0:T(2,128)S(1)} %broadcast_multiply_fusion.1) | copy-start | bytes 12292
Sparse Core Ops, SparseCore 0:
  65.7 51.0 all-gather.1
where the time goes:
time: 266 us; the launch traced here: 265 us
  blocking collectives  128 us (48%)
  waiting for transfers between devices  87.2 us (33%)
  matrix products  20.6 us (8%)
  between operations  15 us (6%)
  starting transfers between devices  6.04 us (2%)
  local copies, waits for them, and re-layouts  5.7 us (2%)
    psum x1, blocking collectives, on_device(): modal_forces = lax.psum(jnp.stack([force_re, force_im]), ('blk', 'face'))  57.6 us
    all_gather x1, waiting for transfers between devices, on_device(): lax.all_gather(panels, 'blk', axis=2, tiled=True)  48.7 us
    ppermute x1, waiting for transfers between devices, shifted(): return lax.ppermute(x, axis, [(i, (i + by) % count) for i in range(count)])  38.5 us
    psum x2, blocking collectives, on_device(): lax.psum(jnp.sum(rows_re * rows_re + rows_im * rows_im, axis=1), 'blk')  36.8 us
    all_gather x1, blocking collectives, on_device(): lax.all_gather(jnp.stack([rows_re, rows_im]), 'blk', axis=2, tiled=True)  30.5 us
    ppermute x1, starting transfers between devices, shifted(): return lax.ppermute(x, axis, [(i, (i + by) % count) for i in range(count)])  6 us
  transfers between devices with their start and end apart: 2, of which 2 were waited for; matrix products, arithmetic and copies ran while one was open for 3% of the time, Pallas kernels for 0%

commit v1 on v0

v1 whole, which is shorter than its diff:
```python
import functools
import math

import jax
import jax.numpy as jnp
import ml_dtypes
import numpy as np
from jax import lax
from jax.experimental import pallas as pl
from jax.experimental.pallas import tpu as pltpu
from jax.sharding import PartitionSpec as P

NFFT = 1024
HOP = 512
BIN = 16
FIRST_BIN = 24
PITERS = 2
BLK_DEV = 2
NTAP = 512
NMODE = 4
NC = 3
ROWS = 8
F_LANE = 64

HIGH = lax.Precision.HIGHEST
NT = (((1,), (1,)), ((), ()))


def band_twiddle():
    steps = np.arange(NFFT)
    bins = FIRST_BIN + np.arange(BIN)
    angle = (steps[:, None] * bins[None, :] % NFFT) * (2.0 * math.pi / NFFT)
    window = 0.5 - 0.5 * np.cos(steps * (2.0 * math.pi / NFFT))
    scaling = np.sqrt(np.sum(window * window))
    cosine = window[:, None] * np.cos(angle) / scaling
    sine = -window[:, None] * np.sin(angle) / scaling
    return np.concatenate([cosine, sine], axis=1).astype(np.float32)


def thirds(x, cast):
    first = x.astype(jnp.bfloat16)
    rest = x - cast(first)
    second = rest.astype(jnp.bfloat16)
    third = (rest - cast(second)).astype(jnp.bfloat16)
    return first, second, third


def message_twiddle():
    twiddle = band_twiddle()
    early, late = twiddle[:HOP].T.reshape(2, BIN, HOP), twiddle[HOP:].T.reshape(2, BIN, HOP)
    rows = np.zeros((BIN, ROWS, 2, HOP), np.float32)
    for part in range(2):
        rows[:, part, 0] = early[part]
        rows[:, part, 1] = late[part]
        rows[:, 2 + part, 1] = early[part]
        rows[:, 4 + part, 0] = late[part]
    rows = rows.reshape(BIN * ROWS, NFFT)
    first = rows.astype(ml_dtypes.bfloat16)
    rest = rows - first.astype(np.float32)
    second = rest.astype(ml_dtypes.bfloat16)
    third = (rest - second.astype(np.float32)).astype(ml_dtypes.bfloat16)
    return np.concatenate([first, second, third], axis=0)


def f32(x):
    return x.astype(jnp.float32)


def spectra_kernel(odd_ref, twiddle_ref, record_ref, area_ref, tap_ref, lever_ref, out_ref):
    m = BIN * ROWS
    first, second, third = thirds(record_ref[...], f32)
    dot = functools.partial(jnp.dot, preferred_element_type=jnp.float32)
    one = dot(twiddle_ref[...], first)
    two = dot(twiddle_ref[: 2 * m], second)
    three = dot(twiddle_ref[:m], third)
    spectra = ((one[2 * m :] + two[m:]) + three) + (one[m : 2 * m] + two[:m]) + one[:m]
    root = jnp.sqrt(f32(area_ref[...]) / 64.0)
    faces = root.shape[1]
    taps = lax.broadcasted_iota(jnp.int32, (NTAP, faces), 0)
    onehot = jnp.where(taps == tap_ref[...], 1.0, 0.0).astype(jnp.bfloat16)
    lever = f32(lever_ref[...]).astype(jnp.bfloat16)
    force = dot(lever, onehot) * root
    odd = odd_ref[0] != 0
    pair = jnp.where(odd, force[2:4], force[0:2])
    out_ref[...] = (spectra * root).reshape(BIN, ROWS, faces)
    out_ref[:, 6:8, :] = jnp.broadcast_to(pair[None], (BIN, 2, faces))


def spectra_call(odd, twiddle, record, area, tap, lever, chunk=256):
    steps, faces = record.shape
    return pl.pallas_call(
        spectra_kernel,
        grid=(faces // chunk,),
        in_specs=[
            pl.BlockSpec(memory_space=pltpu.SMEM),
            pl.BlockSpec(twiddle.shape, lambda i: (0, 0)),
            pl.BlockSpec((steps, chunk), lambda i: (0, i)),
            pl.BlockSpec((1, chunk), lambda i: (0, i)),
            pl.BlockSpec((1, chunk), lambda i: (0, i)),
            pl.BlockSpec(lever.shape, lambda i: (0, 0)),
        ],
        out_specs=pl.BlockSpec((BIN, ROWS, chunk), lambda i: (0, 0, i)),
        out_shape=jax.ShapeDtypeStruct((BIN, ROWS, faces), jnp.float32),
        compiler_params=pltpu.CompilerParams(vmem_limit_bytes=32 * 2**20),
        name="band_spectra",
    )(odd, twiddle, record, area, tap, lever)


def modes_kernel(total_faces, block_count, bin_ref, got_ref, start_ref, out_ref):
    cycle = block_count // BLK_DEV
    dot = functools.partial(lax.dot_general, preferred_element_type=jnp.float32)
    real, imag, force = [], [], []
    for face in range(2):
        got = [got_ref[2 * d + face] for d in range(cycle)]
        rows = ([], [])
        for d in range(cycle):
            for part in range(2):
                rows[part].append(got[d][part : part + 1])
                rows[part].append(got[d][2 + part : 3 + part] + got[(d + 1) % cycle][4 + part : 5 + part])
        real.append(jnp.concatenate(rows[0], axis=0))
        imag.append(jnp.concatenate(rows[1], axis=0))
        force.append(jnp.concatenate([got[0][6:8], got[1][6:7], jnp.zeros_like(got[0][:5])], axis=0))
    real = jnp.concatenate(real, axis=1)
    imag = jnp.concatenate(imag, axis=1)
    force = jnp.concatenate(force, axis=1)
    q = jnp.concatenate([real, imag], axis=0)
    both = dot(jnp.concatenate([q, force], axis=0), q, NT, precision=HIGH)
    n = block_count
    rr, ri = both[:n, :n], both[:n, n : 2 * n]
    ir, ii = both[n : 2 * n, :n], both[n : 2 * n, n : 2 * n]
    gram_re = (rr + ii) / total_faces
    gram_im = (ri - ir) / total_faces
    gram = jnp.concatenate(
        [jnp.concatenate([gram_re, -gram_im], axis=1), jnp.concatenate([gram_im, gram_re], axis=1)], axis=0
    )
    load = both[2 * n :] / math.sqrt(total_faces * block_count)
    own = bin_ref[0]
    modes = jnp.concatenate([start_ref[0, own], start_ref[1, own]], axis=1)
    for _ in range(PITERS):
        new = dot(modes, gram, (((1,), (0,)), ((), ())), precision=HIGH)
        scale = jnp.sqrt(jnp.sum(new * new, axis=1, keepdims=True) / block_count + 1e-06)
        modes = new / scale
    re, im = modes[:, :n], modes[:, n:]
    signed = jnp.concatenate(
        [jnp.concatenate([re, -im], axis=1), jnp.concatenate([im, re], axis=1)], axis=0
    )
    padded = jnp.concatenate([jnp.zeros((F_LANE, 2 * n), jnp.float32), load, jnp.zeros((128 - F_LANE - 8, 2 * n), jnp.float32)], axis=0)
    reply = dot(signed, padded, NT, precision=HIGH)
    for d in range(cycle):
        for face in range(2):
            out_ref[2 * d + face] = reply
            out_ref[2 * d + face, 0:2, 0 : 2 * n] = gram[n + 2 * d : n + 2 * d + 2]


def modes_call(own_bin, got, start, total_faces, block_count):
    return pl.pallas_call(
        functools.partial(modes_kernel, total_faces, block_count),
        in_specs=[pl.BlockSpec(memory_space=pltpu.SMEM), pl.BlockSpec(memory_space=pltpu.VMEM), pl.BlockSpec(memory_space=pltpu.VMEM)],
        out_specs=pl.BlockSpec(memory_space=pltpu.VMEM),
        out_shape=jax.ShapeDtypeStruct((BIN, 8, 128), jnp.float32),
        compiler_params=pltpu.CompilerParams(vmem_limit_bytes=32 * 2**20),
        name="bin_modes",
    )(own_bin, got, start)


def by_bins(record, face_area, face_tap, lever_table, start_modes):
    faces = record.shape[1]
    cycle = lax.axis_size("blk")
    block_count = BLK_DEV * cycle
    place = lax.axis_index("blk")
    odd = jnp.reshape(place % 2, (1,)).astype(jnp.int32)
    own_bin = jnp.reshape(2 * place + lax.axis_index("face"), (1,)).astype(jnp.int32)
    lever = jnp.pad(lever_table.T, ((0, 8 - NC), (0, 0)))
    messages = spectra_call(
        odd, jnp.asarray(message_twiddle()), record, face_area.reshape(1, faces), face_tap.reshape(1, faces), lever
    )
    got = lax.all_to_all(messages, ("blk", "face"), 0, 0, tiled=True)
    replies = modes_call(own_bin, got, start_modes.transpose(0, 1, 3, 2), faces * 2, block_count)
    back = lax.all_to_all(replies, ("blk", "face"), 0, 0, tiled=True)
    n = block_count
    gram_rows = jnp.stack([back[:, 0:2, n : 2 * n], back[:, 0:2, 0:n]])
    forces = jnp.stack([back[:, 0:4, F_LANE : F_LANE + NC], back[:, 4:8, F_LANE : F_LANE + NC]])
    return gram_rows, forces


def shifted(x, axis, by):
    count = lax.axis_size(axis)
    return lax.ppermute(x, axis, [(i, (i + by) % count) for i in range(count)])


def gram_tiles(weighted, others):
    real_tile = jnp.einsum("kif,kjf->kij", weighted[0], others[0], precision=HIGH)
    real_tile = real_tile + jnp.einsum("kif,kjf->kij", weighted[1], others[1], precision=HIGH)
    imag_tile = jnp.einsum("kif,kjf->kij", weighted[0], others[1], precision=HIGH)
    imag_tile = imag_tile - jnp.einsum("kif,kjf->kij", weighted[1], others[0], precision=HIGH)
    return jnp.stack([real_tile, imag_tile])


def by_rows(record, face_area, face_tap, lever_table, start_modes):
    faces = record.shape[1]
    cycle = lax.axis_size("blk")
    block_count = BLK_DEV * cycle
    total_faces = faces * lax.axis_size("face")
    twiddle = jnp.asarray(band_twiddle())
    hops = record.reshape(BLK_DEV, HOP, faces)
    early = jnp.einsum("tk,btf->kbf", twiddle[:HOP], hops, precision=HIGH)
    late = jnp.einsum("tk,btf->kbf", twiddle[HOP:], hops, precision=HIGH)
    following = shifted(late[:, :1], "blk", -1)
    spectra = early + jnp.concatenate([late[:, 1:], following], axis=1)
    panels = jnp.stack([spectra[:BIN], spectra[BIN:]])
    weight = face_area.astype(jnp.float32) / 64.0
    gram_rows = gram_tiles(panels * weight, lax.all_gather(panels, "blk", axis=2, tiled=True))
    gram_rows = lax.psum(gram_rows, "face") / total_faces
    gram = lax.all_gather(gram_rows, "blk", axis=2, tiled=True)
    re, im = start_modes[0], start_modes[1]
    product = functools.partial(jnp.einsum, "kij,kjm->kim", precision=HIGH)
    for _ in range(PITERS):
        re, im = product(gram[0], re) - product(gram[1], im), product(gram[0], im) + product(gram[1], re)
        scale = jnp.sqrt(jnp.sum(re * re + im * im, axis=1, keepdims=True) / block_count + 1e-06)
        re, im = re / scale, im / scale
    own = BLK_DEV * lax.axis_index("blk")
    re = lax.dynamic_slice_in_dim(re, own, BLK_DEV, 1)
    im = lax.dynamic_slice_in_dim(im, own, BLK_DEV, 1)
    onehot = (face_tap[:, None] == jnp.arange(NTAP, dtype=jnp.int32)[None, :]).astype(jnp.float32)
    face_weight = weight[:, None] * jnp.dot(onehot, lever_table.astype(jnp.float32), precision=HIGH)
    load = jnp.einsum("pkbf,fc->pkbc", panels, face_weight, precision=HIGH) / math.sqrt(total_faces * block_count)
    force = functools.partial(jnp.einsum, "kbc,kbm->kmc", precision=HIGH)
    forces = jnp.stack([force(load[0], re) - force(load[1], im), force(load[0], im) + force(load[1], re)])
    return gram_rows, lax.psum(forces, ("blk", "face"))


def solution(mesh):
    fits = mesh.shape["blk"] * mesh.shape["face"] == BIN and mesh.shape["face"] == 2
    return jax.shard_map(
        by_bins if fits else by_rows,
        mesh=mesh,
        in_specs=(P("blk", ("grp", "face")), P("face"), P("face"), P(), P()),
        out_specs=(P(None, "grp", "blk", None), P(None, "grp", None, None)),
        check_vma=False,
    )
```

time: 266 us -> 45.8 us (0.17)
  blocking collectives: 128 us -> 10.8 us
  waiting for transfers between devices: 87.2 us -> 14.5 us
  matrix products: 20.6 us -> 0 us
  between operations: 15 us -> 0.67 us
  Pallas kernels: 0 us -> 5.04 us
    psum x4 -> x0, blocking collectives: 97.8 us -> none  [the longest x1 57.6 us: on_device(): modal_forces = lax.psum(jnp.stack([force_re, force_im]), ('blk', 'face'))]
    all_gather x1 -> x0, waiting for transfers between devices: 48.7 us -> none  [on_device(): lax.all_gather(panels, 'blk', axis=2, tiled=True)]
    ppermute x1 -> x0, waiting for transfers between devices: 38.5 us -> none  [shifted(): return lax.ppermute(x, axis, [(i, (i + by) % count) for i in range(count)])]
    all_gather x1 -> x0, blocking collectives: 30.5 us -> none  [on_device(): lax.all_gather(jnp.stack([rows_re, rows_im]), 'blk', axis=2, tiled=True)]
    dot_general x21 -> x0, matrix products: 20.6 us -> none  [the longest x1 4.89 us: on_device(): jnp.einsum('tk,btf->kbf', twiddle[:HOP], extended[:BLK_DEV], precision=HIGH)]
    all_to_all x0 -> x1, waiting for transfers between devices: none -> 14.5 us  [by_bins(): got = lax.all_to_all(messages, ('blk', 'face'), 0, 0, tiled=True)]
    all_to_all x0 -> x1, blocking collectives: none -> 10.8 us  [by_bins(): back = lax.all_to_all(replies, ('blk', 'face'), 0, 0, tiled=True)]
    all_to_all x0 -> x1, starting transfers between devices: none -> 7.38 us  [by_bins(): got = lax.all_to_all(messages, ('blk', 'face'), 0, 0, tiled=True)]
  transfers between devices with their start and end apart: 2 -> 1, of which waited for: 2 -> 1; matrix products, arithmetic and copies ran while one was open for 3% -> 0% of each run, Pallas kernels for 0% -> 0%
where the time goes in v1:
time: 45.8 us; the launch traced here: 45.4 us
  waiting for transfers between devices  14.5 us (32%)
  blocking collectives  10.8 us (24%)
  starting transfers between devices  7.38 us (16%)
  local copies, waits for them, and re-layouts  5.78 us (13%)
  Pallas kernels  5.04 us (11%)
  other arithmetic  1.25 us (3%)
  between operations  0.67 us (1%)
    all_to_all x1, waiting for transfers between devices, by_bins(): got = lax.all_to_all(messages, ('blk', 'face'), 0, 0, tiled=True)  14.5 us
    all_to_all x1, blocking collectives, by_bins(): back = lax.all_to_all(replies, ('blk', 'face'), 0, 0, tiled=True)  10.8 us
    all_to_all x1, starting transfers between devices, by_bins(): got = lax.all_to_all(messages, ('blk', 'face'), 0, 0, tiled=True)  7.38 us
    unnamed x10, local copies, waits for them, and re-layouts  4.7 us
    pallas_call x1, Pallas kernels, spectra_call(): pl.pallas_call(spectra_kernel, grid=(faces // chunk,), in_specs=[pl.Block...  3.63 us
    pallas_call x1, Pallas kernels, modes_call(): pl.pallas_call(functools.partial(modes_kernel, total_faces, block_count),...  1.41 us
  transfers between devices with their start and end apart: 1, of which 1 were waited for; matrix products, arithmetic and copies ran while one was open for 0% of the time, Pallas kernels for 0%

profile of v1, /device:TPU:0, one launch (start us, length us, event | category | flops | bytes accessed | tf_op | source)
XLA Modules:
  0.0 45.4 jit_solution(7073499890150376663)
XLA Ops:
  0.6 0.7 %pad.4.lever_ref = s32[8,512]{1,0:T(8,128)S(1)} pad(s32[3,512]{1,0:T(4,128)} %bitcast.17, s32[]{:T(128)} %constant.22.clone.1), padding=0_5x0_0 | pad | bytes 22532 | tf_op jit(solution)/shard_map/jit(_pad)/pad | solution.py:173
  1.3 0.0 copy-start
  1.3 2.2 %copy-done = f32[1024,1024]{1,0:T(8,128)S(1)} copy-done((f32[1024,1024]{1,0:T(8,128)S(1)}, f32[1024,1024]{1,0:T(8,128)}, u32[]{:S(2)}) %copy-start) | copy-done | bytes 4194328
  3.5 0.0 copy-start.1
  3.5 1.1 %copy-done.1 = bf16[384,1024]{1,0:T(8,128)(2,1)S(1)} copy-done((bf16[384,1024]{1,0:T(8,128)(2,1)S(1)}, bf16[384,1024]{1,0:T(8,128)(2,1)}, u32[]{:S(2)}) %copy-start.1) | copy-done | bytes 786456
  4.7 0.0 copy-start.3
  4.7 0.7 %copy-done.3 = s32[1024]{0:T(1024)S(1)} copy-done((s32[1024]{0:T(1024)S(1)}, s32[1024]{0:T(1024)}, u32[]{:S(2)}) %copy-start.3) | copy-done | bytes 4120
  5.4 0.0 copy-start.4
  5.4 0.7 %copy-done.4 = s32[1024]{0:T(1024)S(1)} copy-done((s32[1024]{0:T(1024)S(1)}, s32[1024]{0:T(1024)}, u32[]{:S(2)}) %copy-start.4) | copy-done | bytes 4120
  6.0 0.0 copy-start.2
  6.0 3.6 %band_spectra.1 = f32[16,8,1024]{2,1,0:T(8,128)} custom-call(s32[1]{0:T(128)} %bitcast.1.odd_ref, bf16[384,1024]{1,0:T(8,128)(2,1)S(1)} %copy-done.1, f32[1024,1024]{1,0:T(8,128)S(1)} %copy-done, s32[1,1024]{1,0:T(1,128)S(1)} %bitcast.15, s32[1,1024]{1,0:T(1,128)S(1)} %bitcast.16, s32[8,512]{1,0:T(8,128)S(1)} %pad.4.lever_ref), custom_call_target="tpu_custom_call" | custom-call | tf_op jit(solution)/shard_map/band_spectra/pallas_call | solution.py:91
  9.7 7.4 %all-to-all-start = ((f32[16,8,1024]{2,1,0:T(8,128)}), f32[16,8,1024]{2,1,0:T(8,128)S(1)}, u32[]{:S(2)}, u32[]{:S(2)}) async-start(f32[16,8,1024]{2,1,0:T(8,128)} %band_spectra.1), calls=%async_computation | async-start | bytes 1048576 | tf_op jit(solution)/shard_map/all_to_all | solution.py:177
  17.1 14.5 %all-to-all-done.got_ref = f32[16,8,1024]{2,1,0:T(8,128)S(1)} async-done(((f32[16,8,1024]{2,1,0:T(8,128)}), f32[16,8,1024]{2,1,0:T(8,128)S(1)}, u32[]{:S(2)}, u32[]{:S(2)}) %all-to-all-start) | async-done | bytes 524320 | tf_op jit(solution)/shard_map/all_to_all | solution.py:177
  31.5 0.0 copy-done.2
  31.5 1.4 %bin_modes.1 = f32[16,8,128]{2,1,0:T(8,128)S(1)} custom-call(s32[1]{0:T(128)} %bitcast.bin_ref, f32[16,8,1024]{2,1,0:T(8,128)S(1)} %all-to-all-done.got_ref, f32[2,16,4,16]{3,2,1,0:T(4,128)S(1)} %bitcast.14), custom_call_target="tpu_custom_call" | custom-call | tf_op jit(solution)/shard_map/bin_modes/pallas_call | solution.py:156
  32.9 10.8 %all_to_all.10 = f32[16,8,128]{2,1,0:T(8,128)S(1)} all-to-all(f32[16,8,128]{2,1,0:T(8,128)S(1)} %bin_modes.1), channel_id=1, replica_groups=mesh['grp'=2,'blk'=8,'face'=2] {'blk','face'}, dimensions={0} | all-to-all | bytes 131072 | tf_op jit(solution)/shard_map/all_to_all | solution.py:179
  43.8 0.1 slice_bitcast_fusion.1
  43.9 0.1 copy.9
  44.0 0.1 copy.10
  44.1 0.1 slice_bitcast_fusion.3
  44.1 0.6 %pad_maximum_fusion = f32[2,16,2,16]{3,2,1,0:T(2,128)} fusion(f32[1,16,2,16]{3,2,1,0:T(2,128)S(1)} %get-tuple-element.7, f32[1,16,2,16]{3,2,1,0:T(2,128)S(1)} %get-tuple-element.6), kind=kLoop, calls=%fused_computation.2 | loop fusion | flops 1024 | bytes 8192 | tf_op jit(solution)/shard_map/stack | solution.py:181
  44.8 0.6 %pad_maximum_fusion.1 = f32[2,16,4,3]{1,2,3,0:T(4,128)} fusion(f32[1,16,4,3]{1,2,3,0:T(4,128)S(1)} %copy.10, f32[1,16,4,3]{1,2,3,0:T(4,128)S(1)} %copy.9), kind=kLoop, calls=%fused_computation.5 | loop fusion | flops 384 | bytes 3072 | tf_op jit(solution)/shard_map/stack | solution.py:182
Async XLA Ops:
  1.3 2.2 %copy-start = (f32[1024,1024]{1,0:T(8,128)S(1)}, f32[1024,1024]{1,0:T(8,128)}, u32[]{:S(2)}) copy-start(f32[1024,1024]{1,0:T(8,128)} %record_ref.1) | copy-start | bytes 12582916
  3.5 1.1 %copy-start.1 = (bf16[384,1024]{1,0:T(8,128)(2,1)S(1)}, bf16[384,1024]{1,0:T(8,128)(2,1)}, u32[]{:S(2)}) copy-start(bf16[384,1024]{1,0:T(8,128)(2,1)} %constant.24.clone.twiddle_ref) | copy-start | bytes 2359300
  4.7 0.7 %copy-start.3 = (s32[1024]{0:T(1024)S(1)}, s32[1024]{0:T(1024)}, u32[]{:S(2)}) copy-start(s32[1024]{0:T(1024)} %param.7) | copy-start | bytes 12292
  5.4 0.7 %copy-start.4 = (s32[1024]{0:T(1024)S(1)}, s32[1024]{0:T(1024)}, u32[]{:S(2)}) copy-start(s32[1024]{0:T(1024)} %param.8) | copy-start | bytes 12292
  6.0 25.5 %copy-start.2 = (f32[2,16,16,4]{2,3,1,0:T(4,128)S(1)}, f32[2,16,16,4]{2,3,1,0:T(4,128)}, u32[]{:S(2)}) copy-start(f32[2,16,16,4]{2,3,1,0:T(4,128)} %param.10) | copy-start | bytes 24580
  9.7 21.9 %all-to-all-start = ((f32[16,8,1024]{2,1,0:T(8,128)}), f32[16,8,1024]{2,1,0:T(8,128)S(1)}, u32[]{:S(2)}, u32[]{:S(2)}) async-start(f32[16,8,1024]{2,1,0:T(8,128)} %band_spectra.1), calls=%async_computation | async-start | bytes 1048576 | tf_op jit(solution)/shard_map/all_to_all | solution.py:177

commit v2 on v1

v2 whole, which is shorter than its diff:
```python
import functools
import math

import jax
import jax.numpy as jnp
import ml_dtypes
import numpy as np
from jax import lax
from jax.experimental import pallas as pl
from jax.experimental.pallas import tpu as pltpu
from jax.sharding import PartitionSpec as P

NFFT = 1024
HOP = 512
BIN = 16
FIRST_BIN = 24
PITERS = 2
BLK_DEV = 2
NTAP = 512
NMODE = 4
NC = 3
LANES = 128
SPANS = 8
ROWS = 48
SPLIT = 4
F_LANE = 64
VMEM_LIMIT = 60 * 2**20

HIGH = lax.Precision.HIGHEST
NT = (((1,), (1,)), ((), ()))


def band_twiddle():
    steps = np.arange(NFFT)
    bins = FIRST_BIN + np.arange(BIN)
    angle = (steps[:, None] * bins[None, :] % NFFT) * (2.0 * math.pi / NFFT)
    window = 0.5 - 0.5 * np.cos(steps * (2.0 * math.pi / NFFT))
    scaling = np.sqrt(np.sum(window * window))
    cosine = window[:, None] * np.cos(angle) / scaling
    sine = -window[:, None] * np.sin(angle) / scaling
    return np.concatenate([cosine, sine], axis=1).astype(np.float32)


def thirds(x, cast):
    first = x.astype(jnp.bfloat16)
    rest = x - cast(first)
    second = rest.astype(jnp.bfloat16)
    third = (rest - cast(second)).astype(jnp.bfloat16)
    return first, second, third


def folded_twiddle():
    twiddle = band_twiddle().reshape(2, HOP, 2, BIN)
    rows = twiddle.transpose(0, 3, 2, 1).reshape(4 * BIN, HOP)
    first = rows.astype(ml_dtypes.bfloat16)
    rest = rows - first.astype(np.float32)
    second = rest.astype(ml_dtypes.bfloat16)
    third = (rest - second.astype(np.float32)).astype(ml_dtypes.bfloat16)
    return np.concatenate([first, second, third], axis=0)


def f32(x):
    return x.astype(jnp.float32)


def even_row(span):
    return 2 * span


def odd_row(span):
    return ROWS // 2 + 2 * span


def late_row(span):
    return 2 * SPANS + 2 * span if span < SPANS // 2 else ROWS // 2 + SPANS + 2 * span


def spectra_kernel(
    twiddle_hbm, record_hbm, area_hbm, tap_hbm, lever_hbm, out_ref, force_ref, twiddle, record, area, tap, lever, sems, record_sems
):
    faces = record.shape[1]
    width = faces // SPLIT
    small = [
        pltpu.make_async_copy(source, target, sems.at[i])
        for i, (source, target) in enumerate(((area_hbm, area), (tap_hbm, tap), (lever_hbm, lever), (twiddle_hbm, twiddle)))
    ]
    parts = [slice(q * width, (q + 1) * width) for q in range(SPLIT)]
    large = [
        pltpu.make_async_copy(record_hbm.at[:, part], record.at[:, part], record_sems.at[q]) for q, part in enumerate(parts)
    ]
    for copy in small[:3]:
        copy.start()
    small[3].start()
    for copy in large:
        copy.start()
    for copy in small[:3]:
        copy.wait()
    dot = functools.partial(jnp.dot, preferred_element_type=jnp.float32)
    root = jnp.sqrt(f32(area[...]) / 64.0)
    taps = lax.broadcasted_iota(jnp.int32, (NTAP, faces), 0)
    onehot = jnp.where(taps == tap[...], 1.0, 0.0).astype(jnp.bfloat16)
    force_ref[0:NC] = dot(f32(lever[...]).astype(jnp.bfloat16), onehot) * root
    force_ref[NC:] = jnp.zeros((8 - NC, faces), jnp.float32)
    small[3].wait()
    m = 4 * BIN
    for q, part in enumerate(parts):
        large[q].wait()
        halves = []
        for hop in range(BLK_DEV):
            first, second, third = thirds(record[hop * HOP : (hop + 1) * HOP, part], f32)
            one = dot(twiddle[...], first)
            two = dot(twiddle[: 2 * m], second)
            three = dot(twiddle[:m], third)
            halves.append((((one[2 * m :] + two[m:]) + three) + (one[m : 2 * m] + two[:m]) + one[:m]) * root[:, part])
        even = halves[0][: 2 * BIN] + halves[1][2 * BIN :]
        odd = halves[1][: 2 * BIN]
        late = halves[0][2 * BIN :]
        for k in range(BIN):
            pair = slice(2 * k, 2 * k + 2)
            for i in range(width // LANES):
                span, lane = q * (width // LANES) + i, slice(i * LANES, (i + 1) * LANES)
                out_ref[k, even_row(span) : even_row(span) + 2, :] = even[pair, lane]
                out_ref[k, odd_row(span) : odd_row(span) + 2, :] = odd[pair, lane]
                out_ref[k, late_row(span) : late_row(span) + 2, :] = late[pair, lane]


def spectra_call(twiddle, record, area, tap, lever):
    steps, faces = record.shape
    return pl.pallas_call(
        spectra_kernel,
        in_specs=[pl.BlockSpec(memory_space=pl.ANY)] * 5,
        out_specs=[pl.BlockSpec(memory_space=pltpu.VMEM)] * 2,
        out_shape=[
            jax.ShapeDtypeStruct((BIN, ROWS, LANES), jnp.float32),
            jax.ShapeDtypeStruct((8, faces), jnp.float32),
        ],
        scratch_shapes=[
            pltpu.VMEM(twiddle.shape, jnp.bfloat16),
            pltpu.VMEM(record.shape, jnp.float32),
            pltpu.VMEM((1, faces), jnp.int32),
            pltpu.VMEM((1, faces), jnp.int32),
            pltpu.VMEM(lever.shape, jnp.int32),
            pltpu.SemaphoreType.DMA((4,)),
            pltpu.SemaphoreType.DMA((SPLIT,)),
        ],
        compiler_params=pltpu.CompilerParams(vmem_limit_bytes=VMEM_LIMIT),
        name="band_spectra",
    )(twiddle, record, area, tap, lever)


def modes_kernel(total_faces, block_count, place_ref, got_ref, own_force_ref, other_force_ref, start_ref, out_ref):
    n = block_count
    dot = functools.partial(lax.dot_general, preferred_element_type=jnp.float32)
    is_odd = lax.broadcasted_iota(jnp.int32, (n, LANES), 0) % 2 == 1
    columns = []
    for face in range(2):
        base = face * (n // BLK_DEV) * ROWS
        for span in range(SPANS):
            rows = []
            for part in range(2):
                direct = got_ref[pl.ds(base + even_row(span) + part, n, stride=ROWS // 2), :]
                start = late_row(span) + part
                shift = 1 if start < ROWS // 2 else 2
                late = got_ref[pl.ds(base + start % (ROWS // 2), n, stride=ROWS // 2), :]
                rows.append(direct + jnp.where(is_odd, pltpu.roll(late, n - shift, 0), 0.0))
            columns.append(jnp.concatenate(rows, axis=0))
    q_all = jnp.concatenate(columns, axis=1)
    face_one = place_ref[1] != 0
    own, other = own_force_ref[...], other_force_ref[...]
    force = jnp.concatenate([jnp.where(face_one, other, own), jnp.where(face_one, own, other)], axis=1)
    spectra = jnp.concatenate(thirds(q_all, f32), axis=0)
    forces = jnp.concatenate(thirds(jnp.concatenate([force, jnp.zeros_like(force)], axis=0), f32), axis=0)
    both = dot(jnp.concatenate([spectra, forces], axis=0), spectra, NT)
    m = 2 * n
    both = (both[:, 2 * m : 3 * m] + both[:, m : 2 * m]) + both[:, :m]
    square = (both[2 * m : 3 * m] + both[m : 2 * m]) + both[:m]
    load = (both[3 * m + 32 : 3 * m + 40] + both[3 * m + 16 : 3 * m + 24]) + both[3 * m : 3 * m + 8]
    gram_re = (square[:n, :n] + square[n:, n:]) / total_faces
    gram_im = (square[:n, n:] - square[n:, :n]) / total_faces
    gram = jnp.concatenate(
        [jnp.concatenate([gram_re, -gram_im], axis=1), jnp.concatenate([gram_im, gram_re], axis=1)], axis=0
    )
    load = load / math.sqrt(total_faces * block_count)
    modes = jnp.concatenate([start_ref[0, place_ref[0]], start_ref[1, place_ref[0]]], axis=1)
    for _ in range(PITERS):
        new = dot(modes, gram, (((1,), (0,)), ((), ())), precision=HIGH)
        scale = jnp.sqrt(jnp.sum(new * new, axis=1, keepdims=True) / block_count + 1e-06)
        modes = new / scale
    re, im = modes[:, :n], modes[:, n:]
    signed = jnp.concatenate([jnp.concatenate([re, -im], axis=1), jnp.concatenate([im, re], axis=1)], axis=0)
    blank = jnp.zeros((F_LANE, 2 * n), jnp.float32)
    padded = jnp.concatenate([blank, signed, blank[: 128 - F_LANE - 2 * NMODE]], axis=0)
    answer = dot(load, padded, NT, precision=HIGH)
    tail = answer[0:1] + pltpu.roll(answer[1:2], 2 * NMODE, 1) + pltpu.roll(answer[2:3], 4 * NMODE, 1)
    lower = jnp.concatenate([gram[n:], jnp.zeros((n, 128 - m), jnp.float32)], axis=1)
    moved = pltpu.roll(lower, m, 1)
    for d in range(n // BLK_DEV):
        reply = lower[2 * d : 2 * d + 1] + moved[2 * d + 1 : 2 * d + 2] + tail
        for face in range(2):
            out_ref[face * (n // BLK_DEV) + d] = reply


def modes_call(place, got, own_force, other_force, start, total_faces, block_count):
    vmem = pl.BlockSpec(memory_space=pltpu.VMEM)
    return pl.pallas_call(
        functools.partial(modes_kernel, total_faces, block_count),
        in_specs=[pl.BlockSpec(memory_space=pltpu.SMEM), vmem, vmem, vmem, vmem],
        out_specs=vmem,
        out_shape=jax.ShapeDtypeStruct((BIN, 1, 128), jnp.float32),
        compiler_params=pltpu.CompilerParams(vmem_limit_bytes=32 * 2**20),
        name="bin_modes",
    )(place, got, own_force, other_force, start)


def outputs_kernel(block_count, back_ref, gram_ref, forces_ref):
    n = block_count
    back = back_ref[...]
    for part in range(2):
        for row in range(BLK_DEV):
            lane = 2 * n * row + n * (1 - part)
            gram_ref[part, :, row, :] = back[:, lane : lane + n]
    turned = back.T
    for part in range(2):
        for c in range(NC):
            line = F_LANE + 2 * NMODE * c + NMODE * part
            forces_ref[part, c] = turned[line : line + NMODE]


def outputs_call(back, block_count):
    vmem = pl.BlockSpec(memory_space=pltpu.VMEM)
    return pl.pallas_call(
        functools.partial(outputs_kernel, block_count),
        in_specs=[vmem],
        out_specs=[vmem, vmem],
        out_shape=[
            jax.ShapeDtypeStruct((2, BIN, BLK_DEV, block_count), jnp.float32),
            jax.ShapeDtypeStruct((2, NC, NMODE, BIN), jnp.float32),
        ],
        name="outputs",
    )(back)


def by_bins(record, face_area, face_tap, lever_table, start_modes):
    faces = record.shape[1]
    cycle = lax.axis_size("blk")
    block_count = BLK_DEV * cycle
    face = lax.axis_index("face")
    place = jnp.stack([cycle * face + lax.axis_index("blk"), face]).astype(jnp.int32)
    messages, force = spectra_call(
        jnp.asarray(folded_twiddle()), record, face_area.reshape(1, faces), face_tap.reshape(1, faces), lever_table.T
    )
    other_force = shifted(force, "face", 1)
    got = lax.all_to_all(messages, ("face", "blk"), 0, 0, tiled=True)
    replies = modes_call(
        place, got.reshape(BIN * ROWS, LANES), force, other_force, start_modes.transpose(0, 1, 3, 2), faces * 2, block_count
    )
    back = lax.all_to_all(replies, ("face", "blk"), 0, 0, tiled=True)
    gram_rows, forces = outputs_call(back.reshape(BIN, 128), block_count)
    return gram_rows, forces.transpose(0, 3, 2, 1)


def shifted(x, axis, by):
    count = lax.axis_size(axis)
    return lax.ppermute(x, axis, [(i, (i + by) % count) for i in range(count)])


def gram_tiles(weighted, others):
    real_tile = jnp.einsum("kif,kjf->kij", weighted[0], others[0], precision=HIGH)
    real_tile = real_tile + jnp.einsum("kif,kjf->kij", weighted[1], others[1], precision=HIGH)
    imag_tile = jnp.einsum("kif,kjf->kij", weighted[0], others[1], precision=HIGH)
    imag_tile = imag_tile - jnp.einsum("kif,kjf->kij", weighted[1], others[0], precision=HIGH)
    return jnp.stack([real_tile, imag_tile])


def by_rows(record, face_area, face_tap, lever_table, start_modes):
    faces = record.shape[1]
    cycle = lax.axis_size("blk")
    block_count = BLK_DEV * cycle
    total_faces = faces * lax.axis_size("face")
    twiddle = jnp.asarray(band_twiddle())
    hops = record.reshape(BLK_DEV, HOP, faces)
    early = jnp.einsum("tk,btf->kbf", twiddle[:HOP], hops, precision=HIGH)
    late = jnp.einsum("tk,btf->kbf", twiddle[HOP:], hops, precision=HIGH)
    following = shifted(late[:, :1], "blk", -1)
    spectra = early + jnp.concatenate([late[:, 1:], following], axis=1)
    panels = jnp.stack([spectra[:BIN], spectra[BIN:]])
    weight = face_area.astype(jnp.float32) / 64.0
    gram_rows = gram_tiles(panels * weight, lax.all_gather(panels, "blk", axis=2, tiled=True))
    gram_rows = lax.psum(gram_rows, "face") / total_faces
    gram = lax.all_gather(gram_rows, "blk", axis=2, tiled=True)
    re, im = start_modes[0], start_modes[1]
    product = functools.partial(jnp.einsum, "kij,kjm->kim", precision=HIGH)
    for _ in range(PITERS):
        re, im = product(gram[0], re) - product(gram[1], im), product(gram[0], im) + product(gram[1], re)
        scale = jnp.sqrt(jnp.sum(re * re + im * im, axis=1, keepdims=True) / block_count + 1e-06)
        re, im = re / scale, im / scale
    own = BLK_DEV * lax.axis_index("blk")
    re = lax.dynamic_slice_in_dim(re, own, BLK_DEV, 1)
    im = lax.dynamic_slice_in_dim(im, own, BLK_DEV, 1)
    onehot = (face_tap[:, None] == jnp.arange(NTAP, dtype=jnp.int32)[None, :]).astype(jnp.float32)
    face_weight = weight[:, None] * jnp.dot(onehot, lever_table.astype(jnp.float32), precision=HIGH)
    load = jnp.einsum("pkbf,fc->pkbc", panels, face_weight, precision=HIGH) / math.sqrt(total_faces * block_count)
    force = functools.partial(jnp.einsum, "kbc,kbm->kmc", precision=HIGH)
    forces = jnp.stack([force(load[0], re) - force(load[1], im), force(load[0], im) + force(load[1], re)])
    return gram_rows, lax.psum(forces, ("blk", "face"))


def solution(mesh):
    fits = mesh.shape["blk"] * mesh.shape["face"] == BIN and mesh.shape["face"] == 2
    return jax.shard_map(
        by_bins if fits else by_rows,
        mesh=mesh,
        in_specs=(P("blk", ("grp", "face")), P("face"), P("face"), P(), P()),
        out_specs=(P(None, "grp", "blk", None), P(None, "grp", None, None)),
        check_vma=False,
    )
```

time: 45.8 us -> 39.9 us (0.87)
  local copies, waits for them, and re-layouts: 5.78 us -> 0.76 us
  Pallas kernels: 5.04 us -> 8.01 us
  waiting for transfers between devices: 14.5 us -> 12.6 us
  blocking collectives: 10.8 us -> 9.61 us
  other arithmetic: 1.25 us -> 0.07 us
    unnamed x10 -> x4, local copies, waits for them, and re-layouts: 4.7 us -> 0.76 us
    all_to_all x1, waiting for transfers between devices: 14.5 us -> 11.6 us  [by_bins(): got = lax.all_to_all(messages, ('face', 'blk'), 0, 0, tiled=True)]
    pallas_call x1 -> x2, Pallas kernels: 3.63 us -> 6.08 us  [the longest x1 4.62 us: spectra_call(): pl.pallas_call(spectra_kernel, in_specs=[pl.BlockSpec(memory_space=pl.ANY...]
    all_to_all x1, blocking collectives: 10.8 us -> 9.61 us  [by_bins(): back = lax.all_to_all(replies, ('face', 'blk'), 0, 0, tiled=True)]
    another operation x2 -> x1, other arithmetic: 1.25 us -> 0.07 us  [by_bins(): jnp.stack([cycle * face + lax.axis_index('blk'), face]).astype(jnp.int32)]
    ppermute x0 -> x1, waiting for transfers between devices: none -> 1 us  [shifted(): return lax.ppermute(x, axis, [(i, (i + by) % count) for i in range(count)])]
    pad x1 -> x0, local copies, waits for them, and re-layouts: 0.7 us -> none  [by_bins(): lever = jnp.pad(lever_table.T, ((0, 8 - NC), (0, 0)))]
    pallas_call x1, Pallas kernels: 1.41 us -> 1.94 us  [modes_call(): pl.pallas_call(functools.partial(modes_kernel, total_faces, block_count),...]
  transfers between devices with their start and end apart: 1 -> 2, of which waited for: 1 -> 2; matrix products, arithmetic and copies ran while one was open for 0% -> 0% of each run, Pallas kernels for 0% -> 0%
where the time goes in v2:
time: 39.9 us; the launch traced here: 39.6 us
  waiting for transfers between devices  12.6 us (32%)
  blocking collectives  9.61 us (24%)
  Pallas kernels  8.01 us (20%)
  starting transfers between devices  7.81 us (20%)
  local copies, waits for them, and re-layouts  0.76 us (2%)
  between operations  0.68 us (2%)
    all_to_all x1, waiting for transfers between devices, by_bins(): got = lax.all_to_all(messages, ('face', 'blk'), 0, 0, tiled=True)  11.6 us
    all_to_all x1, blocking collectives, by_bins(): back = lax.all_to_all(replies, ('face', 'blk'), 0, 0, tiled=True)  9.61 us
    all_to_all x1, starting transfers between devices, by_bins(): got = lax.all_to_all(messages, ('face', 'blk'), 0, 0, tiled=True)  7.4 us
    pallas_call x1, Pallas kernels, spectra_call(): pl.pallas_call(spectra_kernel, in_specs=[pl.BlockSpec(memory_space=pl.ANY...  4.62 us
    pallas_call x1, Pallas kernels, modes_call(): pl.pallas_call(functools.partial(modes_kernel, total_faces, block_count),...  1.94 us
    pallas_call x1, Pallas kernels, outputs_call(): pl.pallas_call(functools.partial(outputs_kernel, block_count), in_specs=[...  1.46 us
    ppermute x1, waiting for transfers between devices, shifted(): return lax.ppermute(x, axis, [(i, (i + by) % count) for i in range(count)])  1 us
  transfers between devices with their start and end apart: 2, of which 2 were waited for; matrix products, arithmetic and copies ran while one was open for 0% of the time, Pallas kernels for 0%

profile of v2, /device:TPU:0, one launch (start us, length us, event | category | flops | bytes accessed | tf_op | source)
XLA Modules:
  0.0 39.6 jit_solution(17255075384726940835)
XLA Ops:
  0.6 0.0 copy-start
  0.6 4.6 %band_spectra.1 = (f32[16,48,128]{2,1,0:T(8,128)}, f32[8,1024]{1,0:T(8,128)}) custom-call(bf16[192,512]{1,0:T(8,128)(2,1)} %constant.12.clone.twiddle_hbm, f32[1024,1024]{1,0:T(8,128)} %record_hbm.1, s32[1,1024]{1,0:T(1,128)} %bitcast.13, s32[1,1024]{1,0:T(1,128)} %bitcast.14, s32[3,512]{1,0:T(4,128)} %bitcast.12), custom_call_target="tpu_custom_call" | custom-call | tf_op jit(solution)/shard_map/band_spectra/pallas_call | solution.py:129
  5.3 7.4 %all-to-all-start = ((f32[16,48,128]{2,1,0:T(8,128)}), f32[16,48,128]{2,1,0:T(8,128)S(1)}, u32[]{:S(2)}, u32[]{:S(2)}) async-start(f32[16,48,128]{2,1,0:T(8,128)} %get-tuple-element.6), calls=%async_computation | async-start | bytes 786432 | tf_op jit(solution)/shard_map/all_to_all | solution.py:253
  12.7 0.4 %collective-permute-start = (f32[8,1024]{1,0:T(8,128)}, f32[8,1024]{1,0:T(8,128)S(1)}, u32[]{:S(2)}, u32[]{:S(2)}) collective-permute-start(f32[8,1024]{1,0:T(8,128)} %get-tuple-element.7.own_force_ref), channel_id=1, source_target_pairs={{0,1},{1,0},{2,3},{3,2},{4,5},{5,4},{6,7},{7,6},{8,9},{9,8},{10,11... | collective-permute-start | bytes 98312 | tf_op jit(solution)/shard_map/ppermute | solution.py:264
  13.1 0.1 pad_add_fusion.place_ref
  13.2 1.0 %collective-permute-done.other_force_ref = f32[8,1024]{1,0:T(8,128)S(1)} collective-permute-done((f32[8,1024]{1,0:T(8,128)}, f32[8,1024]{1,0:T(8,128)S(1)}, u32[]{:S(2)}, u32[]{:S(2)}) %collective-permute-start) | collective-permute-done | bytes 32800 | tf_op jit(solution)/shard_map/ppermute | solution.py:264
  14.2 11.6 %all-to-all-done = f32[16,48,128]{2,1,0:T(8,128)S(1)} async-done(((f32[16,48,128]{2,1,0:T(8,128)}), f32[16,48,128]{2,1,0:T(8,128)S(1)}, u32[]{:S(2)}, u32[]{:S(2)}) %all-to-all-start) | async-done | bytes 393248 | tf_op jit(solution)/shard_map/all_to_all | solution.py:253
  25.8 0.0 copy-done
  25.8 0.0 copy-start.1
  25.8 0.8 %copy-done.1 = f32[8,1024]{1,0:T(8,128)S(1)} copy-done((f32[8,1024]{1,0:T(8,128)S(1)}, f32[8,1024]{1,0:T(8,128)}, u32[]{:S(2)}) %copy-start.1) | copy-done | bytes 32792
  26.5 1.9 %bin_modes.1 = f32[16,1,128]{2,1,0:T(1,128)S(1)} custom-call(s32[2]{0:T(128)S(1)} %pad_add_fusion.place_ref, f32[768,128]{1,0:T(8,128)S(1)} %bitcast.9, f32[8,1024]{1,0:T(8,128)S(1)} %copy-done.1, f32[8,1024]{1,0:T(8,128)S(1)} %collective-permute-done.other_force_ref, f32[2,16,4,16]{3,2,1,0:T(4,128)S(1)} %bitcast.10), custom_call_target="tpu_custom_call" | custom-call | tf_op jit(solution)/shard_map/bin_modes/pallas_call | solution.py:205
  28.5 9.6 %all_to_all.10 = f32[16,1,128]{2,1,0:T(1,128)} all-to-all(f32[16,1,128]{2,1,0:T(1,128)S(1)} %bin_modes.1), channel_id=1, replica_groups=mesh['grp'=2,'blk'=8,'face'=2] {'face','blk'}, dimensions={0} | all-to-all | bytes 16384 | tf_op jit(solution)/shard_map/all_to_all | solution.py:257
  38.1 1.5 %outputs.1 = (f32[2,16,2,16]{3,2,1,0:T(2,128)}, f32[2,3,4,16]{3,2,1,0:T(4,128)}) custom-call(f32[16,128]{1,0:T(8,128)} %bitcast.11), custom_call_target="tpu_custom_call" | custom-call | tf_op jit(solution)/shard_map/outputs/pallas_call | solution.py:231
Async XLA Ops:
  0.6 25.1 %copy-start = (f32[2,16,16,4]{2,3,1,0:T(4,128)S(1)}, f32[2,16,16,4]{2,3,1,0:T(4,128)}, u32[]{:S(2)}) copy-start(f32[2,16,16,4]{2,3,1,0:T(4,128)} %param.10) | copy-start | bytes 24580
  5.3 20.5 %all-to-all-start = ((f32[16,48,128]{2,1,0:T(8,128)}), f32[16,48,128]{2,1,0:T(8,128)S(1)}, u32[]{:S(2)}, u32[]{:S(2)}) async-start(f32[16,48,128]{2,1,0:T(8,128)} %get-tuple-element.6), calls=%async_computation | async-start | bytes 786432 | tf_op jit(solution)/shard_map/all_to_all | solution.py:253
  12.7 1.5 %collective-permute-start = (f32[8,1024]{1,0:T(8,128)}, f32[8,1024]{1,0:T(8,128)S(1)}, u32[]{:S(2)}, u32[]{:S(2)}) collective-permute-start(f32[8,1024]{1,0:T(8,128)} %get-tuple-element.7.own_force_ref), channel_id=1, source_target_pairs={{0,1},{1,0},{2,3},{3,2},{4,5},{5,4},{6,7},{7,6},{8,9},{9,8},{10,11... | collective-permute-start | bytes 98312 | tf_op jit(solution)/shard_map/ppermute | solution.py:264
  25.8 0.8 %copy-start.1 = (f32[8,1024]{1,0:T(8,128)S(1)}, f32[8,1024]{1,0:T(8,128)}, u32[]{:S(2)}) copy-start(f32[8,1024]{1,0:T(8,128)} %get-tuple-element.7.own_force_ref) | copy-start | bytes 98308

commit v3 on v2

--- a/solution.py
+++ b/solution.py
@@ -22,7 +22,7 @@
 LANES = 128
 SPANS = 8
 ROWS = 48
-SPLIT = 4
+SPLIT = 2
 F_LANE = 64
 VMEM_LIMIT = 60 * 2**20
 
@@ -148,7 +148,7 @@
     )(twiddle, record, area, tap, lever)
 
 
-def modes_kernel(total_faces, block_count, place_ref, got_ref, own_force_ref, other_force_ref, start_ref, out_ref):
+def modes_kernel(total_faces, block_count, got_ref, force_ref, start_ref, out_ref):
     n = block_count
     dot = functools.partial(lax.dot_general, preferred_element_type=jnp.float32)
     is_odd = lax.broadcasted_iota(jnp.int32, (n, LANES), 0) % 2 == 1
@@ -165,34 +165,32 @@
                 rows.append(direct + jnp.where(is_odd, pltpu.roll(late, n - shift, 0), 0.0))
             columns.append(jnp.concatenate(rows, axis=0))
     q_all = jnp.concatenate(columns, axis=1)
-    face_one = place_ref[1] != 0
-    own, other = own_force_ref[...], other_force_ref[...]
-    force = jnp.concatenate([jnp.where(face_one, other, own), jnp.where(face_one, own, other)], axis=1)
-    spectra = jnp.concatenate(thirds(q_all, f32), axis=0)
-    forces = jnp.concatenate(thirds(jnp.concatenate([force, jnp.zeros_like(force)], axis=0), f32), axis=0)
-    both = dot(jnp.concatenate([spectra, forces], axis=0), spectra, NT)
+    force = jnp.concatenate([force_ref[0], force_ref[1]], axis=1)
     m = 2 * n
-    both = (both[:, 2 * m : 3 * m] + both[:, m : 2 * m]) + both[:, :m]
-    square = (both[2 * m : 3 * m] + both[m : 2 * m]) + both[:m]
-    load = (both[3 * m + 32 : 3 * m + 40] + both[3 * m + 16 : 3 * m + 24]) + both[3 * m : 3 * m + 8]
+    both = dot(jnp.concatenate([q_all, force], axis=0), q_all, NT, precision=HIGH)
+    square, load = both[:m], both[m:]
     gram_re = (square[:n, :n] + square[n:, n:]) / total_faces
     gram_im = (square[:n, n:] - square[n:, :n]) / total_faces
     gram = jnp.concatenate(
         [jnp.concatenate([gram_re, -gram_im], axis=1), jnp.concatenate([gram_im, gram_re], axis=1)], axis=0
     )
     load = load / math.sqrt(total_faces * block_count)
-    modes = jnp.concatenate([start_ref[0, place_ref[0]], start_ref[1, place_ref[0]]], axis=1)
-    for _ in range(PITERS):
-        new = dot(modes, gram, (((1,), (0,)), ((), ())), precision=HIGH)
-        scale = jnp.sqrt(jnp.sum(new * new, axis=1, keepdims=True) / block_count + 1e-06)
-        modes = new / scale
+    own = n // BLK_DEV * lax.axis_index("face") + lax.axis_index("blk")
+    modes = jnp.concatenate([start_ref[0, own], start_ref[1, own]], axis=1)
+    columns = [jnp.sum(gram * modes[i : i + 1], axis=1, keepdims=True) for i in range(NMODE)]
+    columns = [y / jnp.sqrt(jnp.sum(y * y, axis=0, keepdims=True) / block_count + 1e-06) for y in columns]
+    modes = jnp.concatenate([jnp.sum(gram * y, axis=0, keepdims=True) for y in columns], axis=0)
+    modes = modes / jnp.sqrt(jnp.sum(modes * modes, axis=1, keepdims=True) / block_count + 1e-06)
     re, im = modes[:, :n], modes[:, n:]
     signed = jnp.concatenate([jnp.concatenate([re, -im], axis=1), jnp.concatenate([im, re], axis=1)], axis=0)
-    blank = jnp.zeros((F_LANE, 2 * n), jnp.float32)
-    padded = jnp.concatenate([blank, signed, blank[: 128 - F_LANE - 2 * NMODE]], axis=0)
-    answer = dot(load, padded, NT, precision=HIGH)
-    tail = answer[0:1] + pltpu.roll(answer[1:2], 2 * NMODE, 1) + pltpu.roll(answer[2:3], 4 * NMODE, 1)
-    lower = jnp.concatenate([gram[n:], jnp.zeros((n, 128 - m), jnp.float32)], axis=1)
+    lane = lax.broadcasted_iota(jnp.int32, (2 * NMODE, LANES), 1)
+    line = lax.broadcasted_iota(jnp.int32, (2 * NMODE, LANES), 0)
+    tail = jnp.zeros((2 * NMODE, LANES), jnp.float32)
+    for c in range(NC):
+        answer = jnp.sum(signed * load[c : c + 1], axis=1, keepdims=True)
+        tail = jnp.where(lane == F_LANE + 2 * NMODE * c + line, answer, tail)
+    tail = jnp.sum(tail, axis=0, keepdims=True)
+    lower = jnp.concatenate([gram[n:], jnp.zeros((n, LANES - m), jnp.float32)], axis=1)
     moved = pltpu.roll(lower, m, 1)
     for d in range(n // BLK_DEV):
         reply = lower[2 * d : 2 * d + 1] + moved[2 * d + 1 : 2 * d + 2] + tail
@@ -200,16 +198,16 @@
             out_ref[face * (n // BLK_DEV) + d] = reply
 
 
-def modes_call(place, got, own_force, other_force, start, total_faces, block_count):
+def modes_call(got, force, start, total_faces, block_count):
     vmem = pl.BlockSpec(memory_space=pltpu.VMEM)
     return pl.pallas_call(
         functools.partial(modes_kernel, total_faces, block_count),
-        in_specs=[pl.BlockSpec(memory_space=pltpu.SMEM), vmem, vmem, vmem, vmem],
+        in_specs=[vmem, vmem, vmem],
         out_specs=vmem,
         out_shape=jax.ShapeDtypeStruct((BIN, 1, 128), jnp.float32),
         compiler_params=pltpu.CompilerParams(vmem_limit_bytes=32 * 2**20),
         name="bin_modes",
-    )(place, got, own_force, other_force, start)
+    )(got, force, start)
 
 
 def outputs_kernel(block_count, back_ref, gram_ref, forces_ref):
@@ -236,6 +234,7 @@
             jax.ShapeDtypeStruct((2, BIN, BLK_DEV, block_count), jnp.float32),
             jax.ShapeDtypeStruct((2, NC, NMODE, BIN), jnp.float32),
         ],
+        compiler_params=pltpu.CompilerParams(vmem_limit_bytes=16 * 2**20),
         name="outputs",
     )(back)
 
@@ -244,15 +243,13 @@
     faces = record.shape[1]
     cycle = lax.axis_size("blk")
     block_count = BLK_DEV * cycle
-    face = lax.axis_index("face")
-    place = jnp.stack([cycle * face + lax.axis_index("blk"), face]).astype(jnp.int32)
     messages, force = spectra_call(
         jnp.asarray(folded_twiddle()), record, face_area.reshape(1, faces), face_tap.reshape(1, faces), lever_table.T
     )
-    other_force = shifted(force, "face", 1)
+    forces = lax.all_gather(force, "face")
     got = lax.all_to_all(messages, ("face", "blk"), 0, 0, tiled=True)
     replies = modes_call(
-        place, got.reshape(BIN * ROWS, LANES), force, other_force, start_modes.transpose(0, 1, 3, 2), faces * 2, block_count
+        got.reshape(BIN * ROWS, LANES), forces, start_modes.transpose(0, 1, 3, 2), faces * 2, block_count
     )
     back = lax.all_to_all(replies, ("face", "blk"), 0, 0, tiled=True)
     gram_rows, forces = outputs_call(back.reshape(BIN, 128), block_count)

time: 39.9 us -> 36 us (0.902)
  Pallas kernels: 8.01 us -> 5.66 us
  waiting for transfers between devices: 12.6 us -> 11 us
  blocking collectives: 9.61 us -> 11 us
  local copies, waits for them, and re-layouts: 0.76 us -> 0.01 us
  starting transfers between devices: 7.81 us -> 7.4 us
    all_gather x0 -> x1, blocking collectives: none -> 2.12 us  [by_bins(): forces = lax.all_gather(force, 'face')]
    pallas_call x1, Pallas kernels: 1.94 us -> 0.91 us  [modes_call(): pl.pallas_call(functools.partial(modes_kernel, total_faces, block_count),...]
    ppermute x1 -> x0, waiting for transfers between devices: 1 us -> none  [shifted(): return lax.ppermute(x, axis, [(i, (i + by) % count) for i in range(count)])]
    unnamed x4 -> x2, local copies, waits for them, and re-layouts: 0.76 us -> 0.01 us
    pallas_call x1, Pallas kernels: 1.46 us -> 0.76 us  [outputs_call(): pl.pallas_call(functools.partial(outputs_kernel, block_count), in_specs=[...]
    all_to_all x1, blocking collectives: 9.61 us -> 8.91 us  [by_bins(): back = lax.all_to_all(replies, ('face', 'blk'), 0, 0, tiled=True)]
    pallas_call x1, Pallas kernels: 4.62 us -> 3.98 us  [spectra_call(): pl.pallas_call(spectra_kernel, in_specs=[pl.BlockSpec(memory_space=pl.ANY...]
    all_to_all x1, waiting for transfers between devices: 11.6 us -> 11 us  [by_bins(): got = lax.all_to_all(messages, ('face', 'blk'), 0, 0, tiled=True)]
  transfers between devices with their start and end apart: 2 -> 1, of which waited for: 2 -> 1; matrix products, arithmetic and copies ran while one was open for 0% -> 0% of each run, Pallas kernels for 0% -> 0%
where the time goes in v3:
time: 36 us; the launch traced here: 35.7 us
  blocking collectives  11 us (31%)
  waiting for transfers between devices  11 us (31%)
  starting transfers between devices  7.4 us (21%)
  Pallas kernels  5.66 us (16%)
  between operations  0.67 us (2%)
    all_to_all x1, waiting for transfers between devices, by_bins(): got = lax.all_to_all(messages, ('face', 'blk'), 0, 0, tiled=True)  11 us
    all_to_all x1, blocking collectives, by_bins(): back = lax.all_to_all(replies, ('face', 'blk'), 0, 0, tiled=True)  8.91 us
    all_to_all x1, starting transfers between devices, by_bins(): got = lax.all_to_all(messages, ('face', 'blk'), 0, 0, tiled=True)  7.4 us
    pallas_call x1, Pallas kernels, spectra_call(): pl.pallas_call(spectra_kernel, in_specs=[pl.BlockSpec(memory_space=pl.ANY...  3.98 us
    all_gather x1, blocking collectives, by_bins(): forces = lax.all_gather(force, 'face')  2.12 us
    pallas_call x1, Pallas kernels, modes_call(): pl.pallas_call(functools.partial(modes_kernel, total_faces, block_count),...  0.91 us
    pallas_call x1, Pallas kernels, outputs_call(): pl.pallas_call(functools.partial(outputs_kernel, block_count), in_specs=[...  0.76 us
  transfers between devices with their start and end apart: 1, of which 1 were waited for; matrix products, arithmetic and copies ran while one was open for 0% of the time, Pallas kernels for 0%

profile of v3, /device:TPU:0, one launch (start us, length us, event | category | flops | bytes accessed | tf_op | source)
XLA Modules:
  0.0 35.7 jit_solution(7768145741534885411)
XLA Ops:
  0.6 0.0 copy-start
  0.6 4.0 %band_spectra.1 = (f32[16,48,128]{2,1,0:T(8,128)}, f32[8,1024]{1,0:T(8,128)}) custom-call(bf16[192,512]{1,0:T(8,128)(2,1)} %constant.2.clone.twiddle_hbm, f32[1024,1024]{1,0:T(8,128)} %record_hbm.1, s32[1,1024]{1,0:T(1,128)} %bitcast.13, s32[1,1024]{1,0:T(1,128)} %bitcast.14, s32[3,512]{1,0:T(4,128)} %bitcast.12), custom_call_target="tpu_custom_call" | custom-call | tf_op jit(solution)/shard_map/band_spectra/pallas_call | solution.py:129
  4.6 7.4 %all-to-all-start = ((f32[16,48,128]{2,1,0:T(8,128)}), f32[16,48,128]{2,1,0:T(8,128)S(1)}, u32[]{:S(2)}, u32[]{:S(2)}) async-start(f32[16,48,128]{2,1,0:T(8,128)} %get-tuple-element.6), calls=%async_computation | async-start | bytes 786432 | tf_op jit(solution)/shard_map/all_to_all | solution.py:250
  12.0 2.1 %all-gather = f32[16,1024]{1,0:T(8,128)S(1)} all-gather(f32[8,1024]{1,0:T(8,128)} %get-tuple-element.7), channel_id=2, replica_groups=mesh['grp'=2,'blk'=8,'face'=2] {'face'}, dimensions={0}, use_global_device_ids=true | all-gather | bytes 98304 | tf_op jit(solution)/shard_map/all_gather | solution.py:249
  14.2 11.0 %all-to-all-done = f32[16,48,128]{2,1,0:T(8,128)S(1)} async-done(((f32[16,48,128]{2,1,0:T(8,128)}), f32[16,48,128]{2,1,0:T(8,128)S(1)}, u32[]{:S(2)}, u32[]{:S(2)}) %all-to-all-start) | async-done | bytes 393248 | tf_op jit(solution)/shard_map/all_to_all | solution.py:250
  25.1 0.0 copy-done
  25.1 0.9 %bin_modes.1 = f32[16,1,128]{2,1,0:T(1,128)S(1)} custom-call(f32[768,128]{1,0:T(8,128)S(1)} %bitcast.8, f32[2,8,1024]{2,1,0:T(8,128)S(1)} %bitcast.9, f32[2,16,4,16]{3,2,1,0:T(4,128)S(1)} %bitcast.10), custom_call_target="tpu_custom_call" | custom-call | tf_op jit(solution)/shard_map/bin_modes/pallas_call | solution.py:203
  26.1 8.9 %all_to_all.10 = f32[16,1,128]{2,1,0:T(1,128)S(1)} all-to-all(f32[16,1,128]{2,1,0:T(1,128)S(1)} %bin_modes.1), channel_id=1, replica_groups=mesh['grp'=2,'blk'=8,'face'=2] {'face','blk'}, dimensions={0} | all-to-all | bytes 16384 | tf_op jit(solution)/shard_map/all_to_all | solution.py:254
  35.0 0.8 %outputs.1 = (f32[2,16,2,16]{3,2,1,0:T(2,128)}, f32[2,3,4,16]{3,2,1,0:T(4,128)}) custom-call(f32[16,128]{1,0:T(8,128)S(1)} %bitcast.11), custom_call_target="tpu_custom_call" | custom-call | tf_op jit(solution)/shard_map/outputs/pallas_call | solution.py:229
Async XLA Ops:
  0.6 24.5 %copy-start = (f32[2,16,16,4]{2,3,1,0:T(4,128)S(1)}, f32[2,16,16,4]{2,3,1,0:T(4,128)}, u32[]{:S(2)}) copy-start(f32[2,16,16,4]{2,3,1,0:T(4,128)} %param.10) | copy-start | bytes 24580
  4.6 20.5 %all-to-all-start = ((f32[16,48,128]{2,1,0:T(8,128)}), f32[16,48,128]{2,1,0:T(8,128)S(1)}, u32[]{:S(2)}, u32[]{:S(2)}) async-start(f32[16,48,128]{2,1,0:T(8,128)} %get-tuple-element.6), calls=%async_computation | async-start | bytes 786432 | tf_op jit(solution)/shard_map/all_to_all | solution.py:250

commit v4 on v3

--- a/solution.py
+++ b/solution.py
@@ -25,6 +25,8 @@
 SPLIT = 2
 F_LANE = 64
 VMEM_LIMIT = 60 * 2**20
+OUT_TURN = 4
+BACK_TURN = 4
 
 HIGH = lax.Precision.HIGHEST
 NT = (((1,), (1,)), ((), ()))
@@ -59,6 +61,15 @@
     return np.concatenate([first, second, third], axis=0)
 
 
+def turned(place, by):
+    cycle = BIN // 2
+    return place // cycle * cycle + (place + by) % cycle
+
+
+def order(turn):
+    return [[turned(place, turn) for place in range(BIN)]]
+
+
 def f32(x):
     return x.astype(jnp.float32)
 
@@ -75,33 +86,19 @@
     return 2 * SPANS + 2 * span if span < SPANS // 2 else ROWS // 2 + SPANS + 2 * span
 
 
-def spectra_kernel(
-    twiddle_hbm, record_hbm, area_hbm, tap_hbm, lever_hbm, out_ref, force_ref, twiddle, record, area, tap, lever, sems, record_sems
-):
+def spectra_kernel(twiddle_hbm, record_hbm, out_ref, twiddle, record, twiddle_sem, record_sems):
     faces = record.shape[1]
     width = faces // SPLIT
-    small = [
-        pltpu.make_async_copy(source, target, sems.at[i])
-        for i, (source, target) in enumerate(((area_hbm, area), (tap_hbm, tap), (lever_hbm, lever), (twiddle_hbm, twiddle)))
-    ]
     parts = [slice(q * width, (q + 1) * width) for q in range(SPLIT)]
+    small = pltpu.make_async_copy(twiddle_hbm.at[: twiddle.shape[0]], twiddle, twiddle_sem)
     large = [
         pltpu.make_async_copy(record_hbm.at[:, part], record.at[:, part], record_sems.at[q]) for q, part in enumerate(parts)
     ]
-    for copy in small[:3]:
-        copy.start()
-    small[3].start()
+    small.start()
     for copy in large:
         copy.start()
-    for copy in small[:3]:
-        copy.wait()
     dot = functools.partial(jnp.dot, preferred_element_type=jnp.float32)
-    root = jnp.sqrt(f32(area[...]) / 64.0)
-    taps = lax.broadcasted_iota(jnp.int32, (NTAP, faces), 0)
-    onehot = jnp.where(taps == tap[...], 1.0, 0.0).astype(jnp.bfloat16)
-    force_ref[0:NC] = dot(f32(lever[...]).astype(jnp.bfloat16), onehot) * root
-    force_ref[NC:] = jnp.zeros((8 - NC, faces), jnp.float32)
-    small[3].wait()
+    small.wait()
     m = 4 * BIN
     for q, part in enumerate(parts):
         large[q].wait()
@@ -111,41 +108,59 @@
             one = dot(twiddle[...], first)
             two = dot(twiddle[: 2 * m], second)
             three = dot(twiddle[:m], third)
-            halves.append((((one[2 * m :] + two[m:]) + three) + (one[m : 2 * m] + two[:m]) + one[:m]) * root[:, part])
+            halves.append(((one[2 * m :] + two[m:]) + three) + (one[m : 2 * m] + two[:m]) + one[:m])
         even = halves[0][: 2 * BIN] + halves[1][2 * BIN :]
         odd = halves[1][: 2 * BIN]
         late = halves[0][2 * BIN :]
         for k in range(BIN):
             pair = slice(2 * k, 2 * k + 2)
+            slot = turned(k, BACK_TURN - OUT_TURN)
             for i in range(width // LANES):
                 span, lane = q * (width // LANES) + i, slice(i * LANES, (i + 1) * LANES)
-                out_ref[k, even_row(span) : even_row(span) + 2, :] = even[pair, lane]
-                out_ref[k, odd_row(span) : odd_row(span) + 2, :] = odd[pair, lane]
-                out_ref[k, late_row(span) : late_row(span) + 2, :] = late[pair, lane]
-
-
-def spectra_call(twiddle, record, area, tap, lever):
+                out_ref[slot, even_row(span) : even_row(span) + 2, :] = even[pair, lane]
+                out_ref[slot, odd_row(span) : odd_row(span) + 2, :] = odd[pair, lane]
+                out_ref[slot, late_row(span) : late_row(span) + 2, :] = late[pair, lane]
+
+
+def spectra_call(twiddle, record):
     steps, faces = record.shape
     return pl.pallas_call(
         spectra_kernel,
-        in_specs=[pl.BlockSpec(memory_space=pl.ANY)] * 5,
-        out_specs=[pl.BlockSpec(memory_space=pltpu.VMEM)] * 2,
-        out_shape=[
-            jax.ShapeDtypeStruct((BIN, ROWS, LANES), jnp.float32),
-            jax.ShapeDtypeStruct((8, faces), jnp.float32),
-        ],
+        in_specs=[pl.BlockSpec(memory_space=pl.ANY)] * 2,
+        out_specs=pl.BlockSpec(memory_space=pltpu.VMEM),
+        out_shape=jax.ShapeDtypeStruct((BIN, ROWS, LANES), jnp.float32),
         scratch_shapes=[
-            pltpu.VMEM(twiddle.shape, jnp.bfloat16),
+            pltpu.VMEM((12 * BIN, HOP), jnp.bfloat16),
             pltpu.VMEM(record.shape, jnp.float32),
-            pltpu.VMEM((1, faces), jnp.int32),
-            pltpu.VMEM((1, faces), jnp.int32),
-            pltpu.VMEM(lever.shape, jnp.int32),
-            pltpu.SemaphoreType.DMA((4,)),
+            pltpu.SemaphoreType.DMA,
             pltpu.SemaphoreType.DMA((SPLIT,)),
         ],
         compiler_params=pltpu.CompilerParams(vmem_limit_bytes=VMEM_LIMIT),
         name="band_spectra",
-    )(twiddle, record, area, tap, lever)
+    )(twiddle, record)
+
+
+def force_kernel(area_ref, tap_ref, lever_ref, out_ref):
+    faces = out_ref.shape[1]
+    root = jnp.sqrt(f32(area_ref[...]) / 64.0)
+    taps = lax.broadcasted_iota(jnp.int32, (NTAP, faces), 0)
+    onehot = jnp.where(taps == tap_ref[...], 1.0, 0.0).astype(jnp.bfloat16)
+    lever = f32(lever_ref[...]).astype(jnp.bfloat16)
+    out_ref[0:NC] = jnp.dot(lever, onehot, preferred_element_type=jnp.float32) * root
+    out_ref[NC : NC + 1] = root
+    out_ref[NC + 1 :] = jnp.zeros((7 - NC, faces), jnp.float32)
+
+
+def force_call(area, tap, lever):
+    vmem = pl.BlockSpec(memory_space=pltpu.VMEM)
+    return pl.pallas_call(
+        force_kernel,
+        in_specs=[vmem, vmem, vmem],
+        out_specs=vmem,
+        out_shape=jax.ShapeDtypeStruct((8, area.shape[1]), jnp.float32),
+        cost_estimate=pl.CostEstimate(flops=2**21, bytes_accessed=2**16, transcendentals=0),
+        name="force_rows",
+    )(area, tap, lever)
 
 
 def modes_kernel(total_faces, block_count, got_ref, force_ref, start_ref, out_ref):
@@ -162,10 +177,10 @@
                 start = late_row(span) + part
                 shift = 1 if start < ROWS // 2 else 2
                 late = got_ref[pl.ds(base + start % (ROWS // 2), n, stride=ROWS // 2), :]
-                rows.append(direct + jnp.where(is_odd, pltpu.roll(late, n - shift, 0), 0.0))
+                rows.append(pltpu.roll(direct + jnp.where(is_odd, pltpu.roll(late, n - shift, 0), 0.0), BLK_DEV * OUT_TURN, 0))
             columns.append(jnp.concatenate(rows, axis=0))
-    q_all = jnp.concatenate(columns, axis=1)
     force = jnp.concatenate([force_ref[0], force_ref[1]], axis=1)
+    q_all = jnp.concatenate(columns, axis=1) * force[NC : NC + 1]
     m = 2 * n
     both = dot(jnp.concatenate([q_all, force], axis=0), q_all, NT, precision=HIGH)
     square, load = both[:m], both[m:]
@@ -175,7 +190,8 @@
         [jnp.concatenate([gram_re, -gram_im], axis=1), jnp.concatenate([gram_im, gram_re], axis=1)], axis=0
     )
     load = load / math.sqrt(total_faces * block_count)
-    own = n // BLK_DEV * lax.axis_index("face") + lax.axis_index("blk")
+    cycle = n // BLK_DEV
+    own = cycle * lax.axis_index("face") + lax.rem(lax.axis_index("blk") + (cycle - BACK_TURN), cycle)
     modes = jnp.concatenate([start_ref[0, own], start_ref[1, own]], axis=1)
     columns = [jnp.sum(gram * modes[i : i + 1], axis=1, keepdims=True) for i in range(NMODE)]
     columns = [y / jnp.sqrt(jnp.sum(y * y, axis=0, keepdims=True) / block_count + 1e-06) for y in columns]
@@ -192,10 +208,10 @@
     tail = jnp.sum(tail, axis=0, keepdims=True)
     lower = jnp.concatenate([gram[n:], jnp.zeros((n, LANES - m), jnp.float32)], axis=1)
     moved = pltpu.roll(lower, m, 1)
-    for d in range(n // BLK_DEV):
+    for d in range(cycle):
         reply = lower[2 * d : 2 * d + 1] + moved[2 * d + 1 : 2 * d + 2] + tail
         for face in range(2):
-            out_ref[face * (n // BLK_DEV) + d] = reply
+            out_ref[turned(face * cycle + d, -BACK_TURN)] = reply
 
 
 def modes_call(got, force, start, total_faces, block_count):
@@ -243,15 +259,14 @@
     faces = record.shape[1]
     cycle = lax.axis_size("blk")
     block_count = BLK_DEV * cycle
-    messages, force = spectra_call(
-        jnp.asarray(folded_twiddle()), record, face_area.reshape(1, faces), face_tap.reshape(1, faces), lever_table.T
-    )
+    messages = spectra_call(jnp.asarray(folded_twiddle()), record)
+    force = force_call(face_area.reshape(1, faces), face_tap.reshape(1, faces), lever_table.T)
     forces = lax.all_gather(force, "face")
-    got = lax.all_to_all(messages, ("face", "blk"), 0, 0, tiled=True)
+    got = lax.all_to_all(messages, ("face", "blk"), 0, 0, tiled=True, axis_index_groups=order(OUT_TURN))
     replies = modes_call(
         got.reshape(BIN * ROWS, LANES), forces, start_modes.transpose(0, 1, 3, 2), faces * 2, block_count
     )
-    back = lax.all_to_all(replies, ("face", "blk"), 0, 0, tiled=True)
+    back = lax.all_to_all(replies, ("face", "blk"), 0, 0, tiled=True, axis_index_groups=order(BACK_TURN))
     gram_rows, forces = outputs_call(back.reshape(BIN, 128), block_count)
     return gram_rows, forces.transpose(0, 3, 2, 1)
 

time: 36 us -> 33.4 us (0.928)
  waiting for transfers between devices: 11 us -> 6.43 us
  Pallas kernels: 5.66 us -> 7.21 us
  starting transfers between devices: 7.4 us -> 7.87 us
    all_to_all x1, waiting for transfers between devices: 11 us -> 6.43 us  [by_bins(): lax.all_to_all(messages, ('face', 'blk'), 0, 0, tiled=True, axis_index_gr...]
    pallas_call x0 -> x1, Pallas kernels: none -> 1.6 us  [force_call(): pl.pallas_call(force_kernel, in_specs=[vmem, vmem, vmem], out_specs=vmem,...]
    all_to_all x1, starting transfers between devices: 7.4 us -> 7.87 us  [by_bins(): lax.all_to_all(messages, ('face', 'blk'), 0, 0, tiled=True, axis_index_gr...]
  transfers between devices with their start and end apart: 1 -> 1, of which waited for: 1 -> 1; matrix products, arithmetic and copies ran while one was open for 0% -> 0% of each run, Pallas kernels for 0% -> 5%
where the time goes in v4:
time: 33.4 us; the launch traced here: 33.1 us
  blocking collectives  10.9 us (33%)
  starting transfers between devices  7.87 us (24%)
  Pallas kernels  7.21 us (22%)
  waiting for transfers between devices  6.43 us (19%)
  between operations  0.67 us (2%)
    all_to_all x1, blocking collectives, by_bins(): lax.all_to_all(replies, ('face', 'blk'), 0, 0, tiled=True, axis_index_gro...  8.86 us
    all_to_all x1, starting transfers between devices, by_bins(): lax.all_to_all(messages, ('face', 'blk'), 0, 0, tiled=True, axis_index_gr...  7.87 us
    all_to_all x1, waiting for transfers between devices, by_bins(): lax.all_to_all(messages, ('face', 'blk'), 0, 0, tiled=True, axis_index_gr...  6.43 us
    pallas_call x1, Pallas kernels, spectra_call(): pl.pallas_call(spectra_kernel, in_specs=[pl.BlockSpec(memory_space=pl.ANY...  3.94 us
    all_gather x1, blocking collectives, by_bins(): forces = lax.all_gather(force, 'face')  2.05 us
    pallas_call x1, Pallas kernels, force_call(): pl.pallas_call(force_kernel, in_specs=[vmem, vmem, vmem], out_specs=vmem,...  1.6 us
    pallas_call x1, Pallas kernels, modes_call(): pl.pallas_call(functools.partial(modes_kernel, total_faces, block_count),...  0.91 us
    pallas_call x1, Pallas kernels, outputs_call(): pl.pallas_call(functools.partial(outputs_kernel, block_count), in_specs=[...  0.76 us
  transfers between devices with their start and end apart: 1, of which 1 were waited for; matrix products, arithmetic and copies ran while one was open for 0% of the time, Pallas kernels for 5%

profile of v4, /device:TPU:0, one launch (start us, length us, event | category | flops | bytes accessed | tf_op | source)
XLA Modules:
  0.0 33.1 jit_solution(3212592110407027987)
XLA Ops:
  0.6 0.0 copy-start
  0.6 3.9 %band_spectra.1 = f32[16,48,128]{2,1,0:T(8,128)} custom-call(bf16[192,512]{1,0:T(8,128)(2,1)} %constant.2.clone.twiddle_hbm, f32[1024,1024]{1,0:T(8,128)} %record_hbm.1), custom_call_target="tpu_custom_call" | custom-call | tf_op jit(solution)/shard_map/band_spectra/pallas_call | solution.py:127
  4.6 7.9 %all-to-all-start = ((f32[16,48,128]{2,1,0:T(8,128)}), f32[16,48,128]{2,1,0:T(8,128)S(1)}, u32[]{:S(2)}, u32[]{:S(2)}) async-start(f32[16,48,128]{2,1,0:T(8,128)} %band_spectra.1), calls=%async_computation | async-start | bytes 786432 | tf_op jit(solution)/shard_map/all_to_all | solution.py:265
  12.5 1.6 %force_rows.1 = f32[8,1024]{1,0:T(8,128)} custom-call(s32[1,1024]{1,0:T(1,128)} %bitcast.13, s32[1,1024]{1,0:T(1,128)} %bitcast.14, s32[3,512]{1,0:T(4,128)} %bitcast.12), custom_call_target="tpu_custom_call" | custom-call | flops 2097152 | bytes 65536 | tf_op jit(solution)/shard_map/force_rows/pallas_call | solution.py:156
  14.1 2.1 %all-gather = f32[16,1024]{1,0:T(8,128)S(1)} all-gather(f32[8,1024]{1,0:T(8,128)} %force_rows.1), channel_id=2, replica_groups=mesh['grp'=2,'blk'=8,'face'=2] {'face'}, dimensions={0}, use_global_device_ids=true | all-gather | bytes 98304 | tf_op jit(solution)/shard_map/all_gather | solution.py:264
  16.1 6.4 %all-to-all-done = f32[16,48,128]{2,1,0:T(8,128)S(1)} async-done(((f32[16,48,128]{2,1,0:T(8,128)}), f32[16,48,128]{2,1,0:T(8,128)S(1)}, u32[]{:S(2)}, u32[]{:S(2)}) %all-to-all-start) | async-done | bytes 393248 | tf_op jit(solution)/shard_map/all_to_all | solution.py:265
  22.5 0.0 copy-done
  22.5 0.9 %bin_modes.1 = f32[16,1,128]{2,1,0:T(1,128)S(1)} custom-call(f32[768,128]{1,0:T(8,128)S(1)} %bitcast.8, f32[2,8,1024]{2,1,0:T(8,128)S(1)} %bitcast.9, f32[2,16,4,16]{3,2,1,0:T(4,128)S(1)} %bitcast.10), custom_call_target="tpu_custom_call" | custom-call | tf_op jit(solution)/shard_map/bin_modes/pallas_call | solution.py:219
  23.5 8.9 %all_to_all.10 = f32[16,1,128]{2,1,0:T(1,128)S(1)} all-to-all(f32[16,1,128]{2,1,0:T(1,128)S(1)} %bin_modes.1), channel_id=1, replica_groups={{8,10,12,14,0,2,4,6,9,11,13,15,1,3,5,7},{24,26,28,30,16,18,20,22,25,27,..., dimensions={0} | all-to-all | bytes 16384 | tf_op jit(solution)/shard_map/all_to_all | solution.py:269
  32.3 0.8 %outputs.1 = (f32[2,16,2,16]{3,2,1,0:T(2,128)}, f32[2,3,4,16]{3,2,1,0:T(4,128)}) custom-call(f32[16,128]{1,0:T(8,128)S(1)} %bitcast.11), custom_call_target="tpu_custom_call" | custom-call | tf_op jit(solution)/shard_map/outputs/pallas_call | solution.py:245
Async XLA Ops:
  0.6 21.9 %copy-start = (f32[2,16,16,4]{2,3,1,0:T(4,128)S(1)}, f32[2,16,16,4]{2,3,1,0:T(4,128)}, u32[]{:S(2)}) copy-start(f32[2,16,16,4]{2,3,1,0:T(4,128)} %param.10) | copy-start | bytes 24580
  4.6 18.0 %all-to-all-start = ((f32[16,48,128]{2,1,0:T(8,128)}), f32[16,48,128]{2,1,0:T(8,128)S(1)}, u32[]{:S(2)}, u32[]{:S(2)}) async-start(f32[16,48,128]{2,1,0:T(8,128)} %band_spectra.1), calls=%async_computation | async-start | bytes 786432 | tf_op jit(solution)/shard_map/all_to_all | solution.py:265

commit v5 on v4

--- a/solution.py
+++ b/solution.py
@@ -25,8 +25,8 @@
 SPLIT = 2
 F_LANE = 64
 VMEM_LIMIT = 60 * 2**20
-OUT_TURN = 4
-BACK_TURN = 4
+TURN = 5
+FIRST_FACE = 1
 
 HIGH = lax.Precision.HIGHEST
 NT = (((1,), (1,)), ((), ()))
@@ -67,7 +67,7 @@
 
 
 def order(turn):
-    return [[turned(place, turn) for place in range(BIN)]]
+    return [[(turned(place, turn) + FIRST_FACE * (BIN // 2)) % BIN for place in range(BIN)]]
 
 
 def f32(x):
@@ -114,12 +114,11 @@
         late = halves[0][2 * BIN :]
         for k in range(BIN):
             pair = slice(2 * k, 2 * k + 2)
-            slot = turned(k, BACK_TURN - OUT_TURN)
             for i in range(width // LANES):
                 span, lane = q * (width // LANES) + i, slice(i * LANES, (i + 1) * LANES)
-                out_ref[slot, even_row(span) : even_row(span) + 2, :] = even[pair, lane]
-                out_ref[slot, odd_row(span) : odd_row(span) + 2, :] = odd[pair, lane]
-                out_ref[slot, late_row(span) : late_row(span) + 2, :] = late[pair, lane]
+                out_ref[k, even_row(span) : even_row(span) + 2, :] = even[pair, lane]
+                out_ref[k, odd_row(span) : odd_row(span) + 2, :] = odd[pair, lane]
+                out_ref[k, late_row(span) : late_row(span) + 2, :] = late[pair, lane]
 
 
 def spectra_call(twiddle, record):
@@ -177,9 +176,9 @@
                 start = late_row(span) + part
                 shift = 1 if start < ROWS // 2 else 2
                 late = got_ref[pl.ds(base + start % (ROWS // 2), n, stride=ROWS // 2), :]
-                rows.append(pltpu.roll(direct + jnp.where(is_odd, pltpu.roll(late, n - shift, 0), 0.0), BLK_DEV * OUT_TURN, 0))
+                rows.append(pltpu.roll(direct + jnp.where(is_odd, pltpu.roll(late, n - shift, 0), 0.0), BLK_DEV * TURN, 0))
             columns.append(jnp.concatenate(rows, axis=0))
-    force = jnp.concatenate([force_ref[0], force_ref[1]], axis=1)
+    force = jnp.concatenate([force_ref[FIRST_FACE], force_ref[1 - FIRST_FACE]], axis=1)
     q_all = jnp.concatenate(columns, axis=1) * force[NC : NC + 1]
     m = 2 * n
     both = dot(jnp.concatenate([q_all, force], axis=0), q_all, NT, precision=HIGH)
@@ -191,7 +190,7 @@
     )
     load = load / math.sqrt(total_faces * block_count)
     cycle = n // BLK_DEV
-    own = cycle * lax.axis_index("face") + lax.rem(lax.axis_index("blk") + (cycle - BACK_TURN), cycle)
+    own = cycle * lax.rem(lax.axis_index("face") + FIRST_FACE, 2) + lax.rem(lax.axis_index("blk") + (cycle - TURN), cycle)
     modes = jnp.concatenate([start_ref[0, own], start_ref[1, own]], axis=1)
     columns = [jnp.sum(gram * modes[i : i + 1], axis=1, keepdims=True) for i in range(NMODE)]
     columns = [y / jnp.sqrt(jnp.sum(y * y, axis=0, keepdims=True) / block_count + 1e-06) for y in columns]
@@ -211,7 +210,7 @@
     for d in range(cycle):
         reply = lower[2 * d : 2 * d + 1] + moved[2 * d + 1 : 2 * d + 2] + tail
         for face in range(2):
-            out_ref[turned(face * cycle + d, -BACK_TURN)] = reply
+            out_ref[turned(face * cycle + d, -TURN)] = reply
 
 
 def modes_call(got, force, start, total_faces, block_count):
@@ -262,11 +261,11 @@
     messages = spectra_call(jnp.asarray(folded_twiddle()), record)
     force = force_call(face_area.reshape(1, faces), face_tap.reshape(1, faces), lever_table.T)
     forces = lax.all_gather(force, "face")
-    got = lax.all_to_all(messages, ("face", "blk"), 0, 0, tiled=True, axis_index_groups=order(OUT_TURN))
+    got = lax.all_to_all(messages, ("face", "blk"), 0, 0, tiled=True, axis_index_groups=order(TURN))
     replies = modes_call(
         got.reshape(BIN * ROWS, LANES), forces, start_modes.transpose(0, 1, 3, 2), faces * 2, block_count
     )
-    back = lax.all_to_all(replies, ("face", "blk"), 0, 0, tiled=True, axis_index_groups=order(BACK_TURN))
+    back = lax.all_to_all(replies, ("face", "blk"), 0, 0, tiled=True, axis_index_groups=order(TURN))
     gram_rows, forces = outputs_call(back.reshape(BIN, 128), block_count)
     return gram_rows, forces.transpose(0, 3, 2, 1)
 

time: 33.4 us -> 32.2 us (0.964)
  waiting for transfers between devices: 6.43 us -> 5.4 us
    all_to_all x1, waiting for transfers between devices: 6.43 us -> 5.4 us  [by_bins(): lax.all_to_all(messages, ('face', 'blk'), 0, 0, tiled=True, axis_index_gr...]
where the time goes in v5:
time: 32.2 us; the launch traced here: 31.9 us
  blocking collectives  10.8 us (34%)
  starting transfers between devices  7.85 us (24%)
  Pallas kernels  7.22 us (22%)
  waiting for transfers between devices  5.4 us (17%)
  between operations  0.67 us (2%)
    all_to_all x1, blocking collectives, by_bins(): lax.all_to_all(replies, ('face', 'blk'), 0, 0, tiled=True, axis_index_gro...  8.71 us
    all_to_all x1, starting transfers between devices, by_bins(): lax.all_to_all(messages, ('face', 'blk'), 0, 0, tiled=True, axis_index_gr...  7.85 us
    all_to_all x1, waiting for transfers between devices, by_bins(): lax.all_to_all(messages, ('face', 'blk'), 0, 0, tiled=True, axis_index_gr...  5.4 us
    pallas_call x1, Pallas kernels, spectra_call(): pl.pallas_call(spectra_kernel, in_specs=[pl.BlockSpec(memory_space=pl.ANY...  3.94 us
    all_gather x1, blocking collectives, by_bins(): forces = lax.all_gather(force, 'face')  2.05 us
    pallas_call x1, Pallas kernels, force_call(): pl.pallas_call(force_kernel, in_specs=[vmem, vmem, vmem], out_specs=vmem,...  1.6 us
    pallas_call x1, Pallas kernels, modes_call(): pl.pallas_call(functools.partial(modes_kernel, total_faces, block_count),...  0.92 us
    pallas_call x1, Pallas kernels, outputs_call(): pl.pallas_call(functools.partial(outputs_kernel, block_count), in_specs=[...  0.76 us
  transfers between devices with their start and end apart: 1, of which 1 were waited for; matrix products, arithmetic and copies ran while one was open for 0% of the time, Pallas kernels for 5%

profile of v5, /device:TPU:0, one launch (start us, length us, event | category | flops | bytes accessed | tf_op | source)
XLA Modules:
  0.0 31.9 jit_solution(7350154632692854652)
XLA Ops:
  0.6 0.0 copy-start
  0.6 3.9 %band_spectra.1 = f32[16,48,128]{2,1,0:T(8,128)} custom-call(bf16[192,512]{1,0:T(8,128)(2,1)} %constant.2.clone.twiddle_hbm, f32[1024,1024]{1,0:T(8,128)} %record_hbm.1), custom_call_target="tpu_custom_call" | custom-call | tf_op jit(solution)/shard_map/band_spectra/pallas_call | solution.py:126
  4.6 7.9 %all-to-all-start = ((f32[16,48,128]{2,1,0:T(8,128)}), f32[16,48,128]{2,1,0:T(8,128)S(1)}, u32[]{:S(2)}, u32[]{:S(2)}) async-start(f32[16,48,128]{2,1,0:T(8,128)} %band_spectra.1), calls=%async_computation | async-start | bytes 786432 | tf_op jit(solution)/shard_map/all_to_all | solution.py:264
  12.4 1.6 %force_rows.1 = f32[8,1024]{1,0:T(8,128)} custom-call(s32[1,1024]{1,0:T(1,128)} %bitcast.13, s32[1,1024]{1,0:T(1,128)} %bitcast.14, s32[3,512]{1,0:T(4,128)} %bitcast.12), custom_call_target="tpu_custom_call" | custom-call | flops 2097152 | bytes 65536 | tf_op jit(solution)/shard_map/force_rows/pallas_call | solution.py:155
  14.0 2.1 %all-gather = f32[16,1024]{1,0:T(8,128)S(1)} all-gather(f32[8,1024]{1,0:T(8,128)} %force_rows.1), channel_id=2, replica_groups=mesh['grp'=2,'blk'=8,'face'=2] {'face'}, dimensions={0}, use_global_device_ids=true | all-gather | bytes 98304 | tf_op jit(solution)/shard_map/all_gather | solution.py:263
  16.1 5.4 %all-to-all-done = f32[16,48,128]{2,1,0:T(8,128)S(1)} async-done(((f32[16,48,128]{2,1,0:T(8,128)}), f32[16,48,128]{2,1,0:T(8,128)S(1)}, u32[]{:S(2)}, u32[]{:S(2)}) %all-to-all-start) | async-done | bytes 393248 | tf_op jit(solution)/shard_map/all_to_all | solution.py:264
  21.5 0.0 copy-done
  21.5 0.9 %bin_modes.1 = f32[16,1,128]{2,1,0:T(1,128)S(1)} custom-call(f32[768,128]{1,0:T(8,128)S(1)} %bitcast.8, f32[2,8,1024]{2,1,0:T(8,128)S(1)} %bitcast.9, f32[2,16,4,16]{3,2,1,0:T(4,128)S(1)} %bitcast.10), custom_call_target="tpu_custom_call" | custom-call | tf_op jit(solution)/shard_map/bin_modes/pallas_call | solution.py:218
  22.4 8.7 %all_to_all.10 = f32[16,1,128]{2,1,0:T(1,128)S(1)} all-to-all(f32[16,1,128]{2,1,0:T(1,128)S(1)} %bin_modes.1), channel_id=1, replica_groups={{11,13,15,1,3,5,7,9,10,12,14,0,2,4,6,8},{27,29,31,17,19,21,23,25,26,28,..., dimensions={0} | all-to-all | bytes 16384 | tf_op jit(solution)/shard_map/all_to_all | solution.py:268
  31.1 0.8 %outputs.1 = (f32[2,16,2,16]{3,2,1,0:T(2,128)}, f32[2,3,4,16]{3,2,1,0:T(4,128)}) custom-call(f32[16,128]{1,0:T(8,128)S(1)} %bitcast.11), custom_call_target="tpu_custom_call" | custom-call | tf_op jit(solution)/shard_map/outputs/pallas_call | solution.py:244
Async XLA Ops:
  0.6 20.9 %copy-start = (f32[2,16,16,4]{2,3,1,0:T(4,128)S(1)}, f32[2,16,16,4]{2,3,1,0:T(4,128)}, u32[]{:S(2)}) copy-start(f32[2,16,16,4]{2,3,1,0:T(4,128)} %param.10) | copy-start | bytes 24580
  4.6 16.9 %all-to-all-start = ((f32[16,48,128]{2,1,0:T(8,128)}), f32[16,48,128]{2,1,0:T(8,128)S(1)}, u32[]{:S(2)}, u32[]{:S(2)}) async-start(f32[16,48,128]{2,1,0:T(8,128)} %band_spectra.1), calls=%async_computation | async-start | bytes 786432 | tf_op jit(solution)/shard_map/all_to_all | solution.py:264

commit v6 on v5

--- a/solution.py
+++ b/solution.py
@@ -27,6 +27,7 @@
 VMEM_LIMIT = 60 * 2**20
 TURN = 5
 FIRST_FACE = 1
+TURNS = (5, 1)
 
 HIGH = lax.Precision.HIGHEST
 NT = (((1,), (1,)), ((), ()))
@@ -68,6 +69,12 @@
 
 def order(turn):
     return [[(turned(place, turn) + FIRST_FACE * (BIN // 2)) % BIN for place in range(BIN)]]
+
+
+def spectra_order():
+    cycle = BIN // 2
+    faces = (FIRST_FACE, 1 - FIRST_FACE)
+    return [[faces[half] * cycle + (place + TURNS[half]) % cycle for half in range(2) for place in range(cycle)]]
 
 
 def f32(x):
@@ -114,11 +121,12 @@
         late = halves[0][2 * BIN :]
         for k in range(BIN):
             pair = slice(2 * k, 2 * k + 2)
+            slot = turned(k, TURN - TURNS[k // (BIN // 2)])
             for i in range(width // LANES):
                 span, lane = q * (width // LANES) + i, slice(i * LANES, (i + 1) * LANES)
-                out_ref[k, even_row(span) : even_row(span) + 2, :] = even[pair, lane]
-                out_ref[k, odd_row(span) : odd_row(span) + 2, :] = odd[pair, lane]
-                out_ref[k, late_row(span) : late_row(span) + 2, :] = late[pair, lane]
+                out_ref[slot, even_row(span) : even_row(span) + 2, :] = even[pair, lane]
+                out_ref[slot, odd_row(span) : odd_row(span) + 2, :] = odd[pair, lane]
+                out_ref[slot, late_row(span) : late_row(span) + 2, :] = late[pair, lane]
 
 
 def spectra_call(twiddle, record):
@@ -176,7 +184,7 @@
                 start = late_row(span) + part
                 shift = 1 if start < ROWS // 2 else 2
                 late = got_ref[pl.ds(base + start % (ROWS // 2), n, stride=ROWS // 2), :]
-                rows.append(pltpu.roll(direct + jnp.where(is_odd, pltpu.roll(late, n - shift, 0), 0.0), BLK_DEV * TURN, 0))
+                rows.append(pltpu.roll(direct + jnp.where(is_odd, pltpu.roll(late, n - shift, 0), 0.0), BLK_DEV * TURNS[face], 0))
             columns.append(jnp.concatenate(rows, axis=0))
     force = jnp.concatenate([force_ref[FIRST_FACE], force_ref[1 - FIRST_FACE]], axis=1)
     q_all = jnp.concatenate(columns, axis=1) * force[NC : NC + 1]
@@ -261,7 +269,7 @@
     messages = spectra_call(jnp.asarray(folded_twiddle()), record)
     force = force_call(face_area.reshape(1, faces), face_tap.reshape(1, faces), lever_table.T)
     forces = lax.all_gather(force, "face")
-    got = lax.all_to_all(messages, ("face", "blk"), 0, 0, tiled=True, axis_index_groups=order(TURN))
+    got = lax.all_to_all(messages, ("face", "blk"), 0, 0, tiled=True, axis_index_groups=spectra_order())
     replies = modes_call(
         got.reshape(BIN * ROWS, LANES), forces, start_modes.transpose(0, 1, 3, 2), faces * 2, block_count
     )

time: 32.2 us -> 32.2 us (level)
  no operation moved by 1% of the time
where the time goes in v6:
time: 32.2 us; the launch traced here: 31.9 us
  blocking collectives  10.7 us (33%)
  starting transfers between devices  7.88 us (24%)
  Pallas kernels  7.22 us (22%)
  waiting for transfers between devices  5.49 us (17%)
  between operations  0.67 us (2%)
    all_to_all x1, blocking collectives, by_bins(): lax.all_to_all(replies, ('face', 'blk'), 0, 0, tiled=True, axis_index_gro...  8.6 us
    all_to_all x1, starting transfers between devices, by_bins(): lax.all_to_all(messages, ('face', 'blk'), 0, 0, tiled=True, axis_index_gr...  7.88 us
    all_to_all x1, waiting for transfers between devices, by_bins(): lax.all_to_all(messages, ('face', 'blk'), 0, 0, tiled=True, axis_index_gr...  5.49 us
    pallas_call x1, Pallas kernels, spectra_call(): pl.pallas_call(spectra_kernel, in_specs=[pl.BlockSpec(memory_space=pl.ANY...  3.94 us
    all_gather x1, blocking collectives, by_bins(): forces = lax.all_gather(force, 'face')  2.05 us
    pallas_call x1, Pallas kernels, force_call(): pl.pallas_call(force_kernel, in_specs=[vmem, vmem, vmem], out_specs=vmem,...  1.6 us
    pallas_call x1, Pallas kernels, modes_call(): pl.pallas_call(functools.partial(modes_kernel, total_faces, block_count),...  0.92 us
    pallas_call x1, Pallas kernels, outputs_call(): pl.pallas_call(functools.partial(outputs_kernel, block_count), in_specs=[...  0.76 us
  transfers between devices with their start and end apart: 1, of which 1 were waited for; matrix products, arithmetic and copies ran while one was open for 0% of the time, Pallas kernels for 5%

profile of v6, /device:TPU:0, one launch (start us, length us, event | category | flops | bytes accessed | tf_op | source)
XLA Modules:
  0.0 31.9 jit_solution(1772314127237140777)
XLA Ops:
  0.6 0.0 copy-start
  0.6 3.9 %band_spectra.1 = f32[16,48,128]{2,1,0:T(8,128)} custom-call(bf16[192,512]{1,0:T(8,128)(2,1)} %constant.2.clone.twiddle_hbm, f32[1024,1024]{1,0:T(8,128)} %record_hbm.1), custom_call_target="tpu_custom_call" | custom-call | tf_op jit(solution)/shard_map/band_spectra/pallas_call | solution.py:134
  4.6 7.9 %all-to-all-start = ((f32[16,48,128]{2,1,0:T(8,128)}), f32[16,48,128]{2,1,0:T(8,128)S(1)}, u32[]{:S(2)}, u32[]{:S(2)}) async-start(f32[16,48,128]{2,1,0:T(8,128)} %band_spectra.1), calls=%async_computation | async-start | bytes 786432 | tf_op jit(solution)/shard_map/all_to_all | solution.py:272
  12.5 1.6 %force_rows.1 = f32[8,1024]{1,0:T(8,128)} custom-call(s32[1,1024]{1,0:T(1,128)} %bitcast.13, s32[1,1024]{1,0:T(1,128)} %bitcast.14, s32[3,512]{1,0:T(4,128)} %bitcast.12), custom_call_target="tpu_custom_call" | custom-call | flops 2097152 | bytes 65536 | tf_op jit(solution)/shard_map/force_rows/pallas_call | solution.py:163
  14.1 2.1 %all-gather = f32[16,1024]{1,0:T(8,128)S(1)} all-gather(f32[8,1024]{1,0:T(8,128)} %force_rows.1), channel_id=2, replica_groups=mesh['grp'=2,'blk'=8,'face'=2] {'face'}, dimensions={0}, use_global_device_ids=true | all-gather | bytes 98304 | tf_op jit(solution)/shard_map/all_gather | solution.py:271
  16.1 5.5 %all-to-all-done = f32[16,48,128]{2,1,0:T(8,128)S(1)} async-done(((f32[16,48,128]{2,1,0:T(8,128)}), f32[16,48,128]{2,1,0:T(8,128)S(1)}, u32[]{:S(2)}, u32[]{:S(2)}) %all-to-all-start) | async-done | bytes 393248 | tf_op jit(solution)/shard_map/all_to_all | solution.py:272
  21.6 0.0 copy-done
  21.6 0.9 %bin_modes.1 = f32[16,1,128]{2,1,0:T(1,128)S(1)} custom-call(f32[768,128]{1,0:T(8,128)S(1)} %bitcast.8, f32[2,8,1024]{2,1,0:T(8,128)S(1)} %bitcast.9, f32[2,16,4,16]{3,2,1,0:T(4,128)S(1)} %bitcast.10), custom_call_target="tpu_custom_call" | custom-call | tf_op jit(solution)/shard_map/bin_modes/pallas_call | solution.py:226
  22.5 8.6 %all_to_all.10 = f32[16,1,128]{2,1,0:T(1,128)S(1)} all-to-all(f32[16,1,128]{2,1,0:T(1,128)S(1)} %bin_modes.1), channel_id=1, replica_groups={{11,13,15,1,3,5,7,9,10,12,14,0,2,4,6,8},{27,29,31,17,19,21,23,25,26,28,..., dimensions={0} | all-to-all | bytes 16384 | tf_op jit(solution)/shard_map/all_to_all | solution.py:276
  31.1 0.8 %outputs.1 = (f32[2,16,2,16]{3,2,1,0:T(2,128)}, f32[2,3,4,16]{3,2,1,0:T(4,128)}) custom-call(f32[16,128]{1,0:T(8,128)S(1)} %bitcast.11), custom_call_target="tpu_custom_call" | custom-call | tf_op jit(solution)/shard_map/outputs/pallas_call | solution.py:252
Async XLA Ops:
  0.6 21.0 %copy-start = (f32[2,16,16,4]{2,3,1,0:T(4,128)S(1)}, f32[2,16,16,4]{2,3,1,0:T(4,128)}, u32[]{:S(2)}) copy-start(f32[2,16,16,4]{2,3,1,0:T(4,128)} %param.10) | copy-start | bytes 24580
  4.6 17.0 %all-to-all-start = ((f32[16,48,128]{2,1,0:T(8,128)}), f32[16,48,128]{2,1,0:T(8,128)S(1)}, u32[]{:S(2)}, u32[]{:S(2)}) async-start(f32[16,48,128]{2,1,0:T(8,128)} %band_spectra.1), calls=%async_computation | async-start | bytes 786432 | tf_op jit(solution)/shard_map/all_to_all | solution.py:272

commit v7 on v6

--- a/solution.py
+++ b/solution.py
@@ -27,7 +27,7 @@
 VMEM_LIMIT = 60 * 2**20
 TURN = 5
 FIRST_FACE = 1
-TURNS = (5, 1)
+TURNS = (5, 2)
 
 HIGH = lax.Precision.HIGHEST
 NT = (((1,), (1,)), ((), ()))
@@ -165,6 +165,7 @@
         in_specs=[vmem, vmem, vmem],
         out_specs=vmem,
         out_shape=jax.ShapeDtypeStruct((8, area.shape[1]), jnp.float32),
+        compiler_params=pltpu.CompilerParams(vmem_limit_bytes=16 * 2**20),
         cost_estimate=pl.CostEstimate(flops=2**21, bytes_accessed=2**16, transcendentals=0),
         name="force_rows",
     )(area, tap, lever)

time: 32.2 us -> 31.6 us (0.981)
  waiting for transfers between devices: 5.49 us -> 6.9 us
  Pallas kernels: 7.22 us -> 5.88 us
  blocking collectives: 10.7 us -> 9.93 us
    all_to_all x1, waiting for transfers between devices: 5.49 us -> 6.9 us  [by_bins(): lax.all_to_all(messages, ('face', 'blk'), 0, 0, tiled=True, axis_index_gr...]
    pallas_call x1, Pallas kernels: 1.6 us -> 0.26 us  [force_call(): pl.pallas_call(force_kernel, in_specs=[vmem, vmem, vmem], out_specs=vmem,...]
    all_to_all x1, blocking collectives: 8.6 us -> 8.09 us  [by_bins(): lax.all_to_all(replies, ('face', 'blk'), 0, 0, tiled=True, axis_index_gro...]
  transfers between devices with their start and end apart: 1 -> 1, of which waited for: 1 -> 1; matrix products, arithmetic and copies ran while one was open for 0% -> 0% of each run, Pallas kernels for 5% -> 1%
where the time goes in v7:
time: 31.6 us; the launch traced here: 31.3 us
  blocking collectives  9.93 us (31%)
  starting transfers between devices  7.88 us (25%)
  waiting for transfers between devices  6.9 us (22%)
  Pallas kernels  5.88 us (19%)
  between operations  0.71 us (2%)
    all_to_all x1, blocking collectives, by_bins(): lax.all_to_all(replies, ('face', 'blk'), 0, 0, tiled=True, axis_index_gro...  8.09 us
    all_to_all x1, starting transfers between devices, by_bins(): lax.all_to_all(messages, ('face', 'blk'), 0, 0, tiled=True, axis_index_gr...  7.88 us
    all_to_all x1, waiting for transfers between devices, by_bins(): lax.all_to_all(messages, ('face', 'blk'), 0, 0, tiled=True, axis_index_gr...  6.9 us
    pallas_call x1, Pallas kernels, spectra_call(): pl.pallas_call(spectra_kernel, in_specs=[pl.BlockSpec(memory_space=pl.ANY...  3.94 us
    all_gather x1, blocking collectives, by_bins(): forces = lax.all_gather(force, 'face')  1.84 us
    pallas_call x1, Pallas kernels, modes_call(): pl.pallas_call(functools.partial(modes_kernel, total_faces, block_count),...  0.92 us
    pallas_call x1, Pallas kernels, outputs_call(): pl.pallas_call(functools.partial(outputs_kernel, block_count), in_specs=[...  0.76 us
  transfers between devices with their start and end apart: 1, of which 1 were waited for; matrix products, arithmetic and copies ran while one was open for 0% of the time, Pallas kernels for 1%

profile of v7, /device:TPU:0, one launch (start us, length us, event | category | flops | bytes accessed | tf_op | source)
XLA Modules:
  0.0 31.3 jit_solution(15483256452019716969)
XLA Ops:
  0.6 0.0 copy-start.2
  0.6 0.0 copy-start.3
  0.7 0.0 copy-start.1
  0.7 0.0 copy-start
  0.7 3.9 %band_spectra.1 = f32[16,48,128]{2,1,0:T(8,128)} custom-call(bf16[192,512]{1,0:T(8,128)(2,1)} %constant.2.clone.twiddle_hbm, f32[1024,1024]{1,0:T(8,128)} %record_hbm.1), custom_call_target="tpu_custom_call" | custom-call | tf_op jit(solution)/shard_map/band_spectra/pallas_call | solution.py:134
  4.6 7.9 %all-to-all-start = ((f32[16,48,128]{2,1,0:T(8,128)}), f32[16,48,128]{2,1,0:T(8,128)S(1)}, u32[]{:S(2)}, u32[]{:S(2)}) async-start(f32[16,48,128]{2,1,0:T(8,128)} %band_spectra.1), calls=%async_computation | async-start | bytes 786432 | tf_op jit(solution)/shard_map/all_to_all | solution.py:273
  12.5 0.0 copy-done.2
  12.5 0.0 copy-done.3
  12.5 0.0 copy-done.1
  12.5 0.3 force_rows.1
  12.8 1.8 %all-gather = f32[16,1024]{1,0:T(8,128)S(1)} all-gather(f32[8,1024]{1,0:T(8,128)S(1)} %force_rows.1), channel_id=2, replica_groups=mesh['grp'=2,'blk'=8,'face'=2] {'face'}, dimensions={0}, use_global_device_ids=true | all-gather | bytes 98304 | tf_op jit(solution)/shard_map/all_gather | solution.py:272
  14.6 6.9 %all-to-all-done = f32[16,48,128]{2,1,0:T(8,128)S(1)} async-done(((f32[16,48,128]{2,1,0:T(8,128)}), f32[16,48,128]{2,1,0:T(8,128)S(1)}, u32[]{:S(2)}, u32[]{:S(2)}) %all-to-all-start) | async-done | bytes 393248 | tf_op jit(solution)/shard_map/all_to_all | solution.py:273
  21.5 0.0 copy-done
  21.5 0.9 %bin_modes.1 = f32[16,1,128]{2,1,0:T(1,128)S(1)} custom-call(f32[768,128]{1,0:T(8,128)S(1)} %bitcast.8, f32[2,8,1024]{2,1,0:T(8,128)S(1)} %bitcast.9, f32[2,16,4,16]{3,2,1,0:T(4,128)S(1)} %bitcast.10), custom_call_target="tpu_custom_call" | custom-call | tf_op jit(solution)/shard_map/bin_modes/pallas_call | solution.py:227
  22.5 8.1 %all_to_all.10 = f32[16,1,128]{2,1,0:T(1,128)S(1)} all-to-all(f32[16,1,128]{2,1,0:T(1,128)S(1)} %bin_modes.1), channel_id=1, replica_groups={{11,13,15,1,3,5,7,9,10,12,14,0,2,4,6,8},{27,29,31,17,19,21,23,25,26,28,..., dimensions={0} | all-to-all | bytes 16384 | tf_op jit(solution)/shard_map/all_to_all | solution.py:277
  30.6 0.8 %outputs.1 = (f32[2,16,2,16]{3,2,1,0:T(2,128)}, f32[2,3,4,16]{3,2,1,0:T(4,128)}) custom-call(f32[16,128]{1,0:T(8,128)S(1)} %bitcast.11), custom_call_target="tpu_custom_call" | custom-call | tf_op jit(solution)/shard_map/outputs/pallas_call | solution.py:253
Async XLA Ops:
  0.6 11.9 %copy-start.2 = (s32[1024]{0:T(1024)S(1)}, s32[1024]{0:T(1024)}, u32[]{:S(2)}) copy-start(s32[1024]{0:T(1024)} %param.7) | copy-start | bytes 12292
  0.6 11.9 %copy-start.3 = (s32[1024]{0:T(1024)S(1)}, s32[1024]{0:T(1024)}, u32[]{:S(2)}) copy-start(s32[1024]{0:T(1024)} %param.8) | copy-start | bytes 12292
  0.7 11.9 %copy-start.1 = (s32[512,3]{0,1:T(4,128)S(1)}, s32[512,3]{0,1:T(4,128)}, u32[]{:S(2)}) copy-start(s32[512,3]{0,1:T(4,128)} %param.9) | copy-start | bytes 18436
  0.7 20.9 %copy-start = (f32[2,16,16,4]{2,3,1,0:T(4,128)S(1)}, f32[2,16,16,4]{2,3,1,0:T(4,128)}, u32[]{:S(2)}) copy-start(f32[2,16,16,4]{2,3,1,0:T(4,128)} %param.10) | copy-start | bytes 24580
  4.6 16.9 %all-to-all-start = ((f32[16,48,128]{2,1,0:T(8,128)}), f32[16,48,128]{2,1,0:T(8,128)S(1)}, u32[]{:S(2)}, u32[]{:S(2)}) async-start(f32[16,48,128]{2,1,0:T(8,128)} %band_spectra.1), calls=%async_computation | async-start | bytes 786432 | tf_op jit(solution)/shard_map/all_to_all | solution.py:273
